TPU v7x, 256 devices: a whole 4x4x8 slice. The times are simulated.
256 devices in a mesh: rows: 32 (over y, z), rrep: 8 (over x, core).
Axes of the slice: x: 4, y: 4, z: 8, core: 2. Of those that a mesh axis runs over, the one named last changes fastest.
Arguments:
- features: bfloat16 [49152, 1024], P(('rows', 'rrep')), may hold values from -6 to 6
- labels: int32 [49152], P(('rows', 'rrep')), may hold values from 0 to 999
- scores: bfloat16 [49152, 1000], P(('rows', 'rrep')), may hold values from -4 to 4
- landmarks: bfloat16 [16384, 1024], P('rows'), may hold values from -6 to 6
- coefficients: float32 [16384, 1000], P('rows'), may hold values from -4 to 4
- block_ids: int32 [2], replicated, may hold values from 0 to 31
Outputs:
- new_coefficients: float32 [16384, 1000], P('rows')
- residual: float32 [49152, 1000], P(('rows', 'rrep'))
Inputs may be any that keep to these rules, and one draw needn't show every extreme that they name: `block_ids`: index of a landmark block; blocks may repeat.
All inputs are finite; a program needn't handle non-finite values.
Results may differ from a plain program's by a relative error of at most 0.003.
Values may be sent and summed in bfloat16 or wider, within the bound.
A program may use at most 128 MiB of HBM per device.

v0:
```python
import jax
import jax.numpy as jnp
from jax import lax
from jax.sharding import PartitionSpec as P


def spread(value, axis, root):
    mine = lax.axis_index(axis) == root
    return lax.psum(jnp.where(mine, value, jnp.zeros_like(value)), axis)


def unit_normalize(values):
    wide = values.astype(jnp.float32)
    scale = lax.rsqrt(jnp.mean(wide * wide, axis=1, keepdims=True) + 1e-06)
    return (wide * scale).astype(jnp.bfloat16)


def contract(left, right):
    return lax.dot_general(
        left, right, (((0,), (0,)), ((), ())), preferred_element_type=jnp.float32
    )


def ridge_solve(gram, product, ridge):
    cholesky_factor = jnp.linalg.cholesky(gram + ridge)
    return jax.scipy.linalg.cho_solve((cholesky_factor, True), product)


def shards(features, labels, scores, landmarks, coefficients, block_ids):
    feature_estimate = unit_normalize(features)
    zhat = unit_normalize(landmarks)
    width = features.shape[1]
    count = coefficients.shape[1]
    size_block = landmarks.shape[0]
    devices_all = lax.axis_size("rows") * lax.axis_size("rrep")
    total_rows = features.shape[0] * devices_all
    ridge = jnp.float32(total_rows) * jnp.eye(size_block, dtype=jnp.float32)
    classes = jnp.arange(count, dtype=jnp.int32)
    residual = (labels[:, None] == classes[None, :]).astype(jnp.float32) - scores.astype(
        jnp.float32
    )
    holder = lax.axis_index("rows")
    steps_count = block_ids.shape[0]
    kernels = []
    for step in range(steps_count):
        landmark_slab = spread(zhat, "rows", block_ids[step])
        inner_product = lax.dot_general(
            feature_estimate,
            landmark_slab,
            (((1,), (1,)), ((), ())),
            preferred_element_type=jnp.float32,
        )
        kernels.append(jnp.exp(inner_product * width ** (-0.5)).astype(jnp.bfloat16))
    new_coefficients = coefficients
    for step in range(steps_count):
        kern = kernels[step]
        rounded = residual.astype(jnp.bfloat16)
        stacked = jnp.concatenate([contract(kern, kern), contract(kern, rounded)], axis=1)
        summed = lax.psum(stacked, ("rows", "rrep"))
        delta = ridge_solve(summed[:, :size_block], summed[:, size_block:], ridge)
        new_coefficients = new_coefficients + jnp.where(holder == block_ids[step], delta, 0.0)
        residual = residual - jnp.dot(
            kern, delta.astype(jnp.bfloat16), preferred_element_type=jnp.float32
        )
    return (new_coefficients, residual)


def solution(mesh):
    in_specs = (
        P(("rows", "rrep"), None),
        P(("rows", "rrep")),
        P(("rows", "rrep"), None),
        P("rows", None),
        P("rows", None),
        P(),
    )
    out_specs = (P("rows", None), P(("rows", "rrep"), None))
    return jax.shard_map(shards, mesh=mesh, in_specs=in_specs, out_specs=out_specs, check_vma=False)
```

profile of v0, /device:TPU:1, one launch (start us, length us, event | category | flops | bytes accessed | tf_op | source)
XLA Modules:
  0.0 1051.5 jit_solution(16937889629836886315)
XLA Ops:
  9.8 1.5 fusion
  11.4 3.1 broadcast_select_fusion.1
  14.7 154.0 %all-reduce.10.cloned.1.call-done = (bf16[512,1024]{1,0:T(8,128)(2,1)}, bf16[512,1024]{1,0:T(8,128)(2,1)}) async-done(((bf16[512,1024]{1,0:T(8,128)(2,1)}, bf16[512,1024]{1,0:T(8,128)(2,1)}), (bf16[512,1024]{1,0:T(8,128)(2,1)}, bf16[512,1024]{1,0:T(8,128)(2,1)})) %all-reduce.10.cloned.1.call-update) | async-done | bytes 2097168 | tf_op jit(solution)/shard_map/psum | solution.py:9
  168.7 1.7 fusion.42
  171.4 2.0 pad_maximum_fusion
  176.5 262.7 %all-reduce.6.cloned.1.call-done = f32[512,1512]{0,1:T(8,128)} async-done(((f32[512,1512]{0,1:T(8,128)}), f32[512,1512]{0,1:T(8,128)}) %all-reduce.6.cloned.1.call-update) | async-done | bytes 3096592 | tf_op jit(solution)/shard_map/psum | solution.py:59
  442.3 11.7 %cholesky.286 = f32[128,128]{1,0:T(8,128)S(1)} custom-call(f32[128,128]{1,0:T(8,128)S(1)} %cholesky.426), custom_call_target="Cholesky" | custom-call | tf_op jit(solution)/shard_map/jit(cholesky)/cholesky | solution.py:25
  454.1 9.8 custom-call.29
  464.7 11.7 %cholesky.305 = f32[128,128]{1,0:T(8,128)S(1)} custom-call(f32[128,128]{1,0:T(8,128)S(1)} %cholesky.430), custom_call_target="Cholesky" | custom-call | tf_op jit(solution)/shard_map/jit(cholesky)/cholesky | solution.py:25
  476.4 10.2 custom-call.30
  487.3 11.7 %cholesky.326 = f32[128,128]{1,0:T(8,128)S(1)} custom-call(f32[128,128]{1,0:T(8,128)S(1)} %cholesky.435), custom_call_target="Cholesky" | custom-call | tf_op jit(solution)/shard_map/jit(cholesky)/cholesky | solution.py:25
  499.8 9.8 custom-call.31
  510.2 11.9 %cholesky.343 = f32[128,128]{1,0:T(8,128)S(1)} custom-call(f32[128,128]{1,0:T(8,128)S(1)} %convolution_subtract_fusion.15), custom_call_target="Cholesky" | custom-call | tf_op jit(solution)/shard_map/jit(cholesky)/cholesky | solution.py:25
  526.3 8.6 while.4
  527.0 1.5 bitcast_dynamic-update-slice_fusion.4
  529.1 1.5 bitcast_dynamic-update-slice_fusion.4
  534.9 39.3 %custom-call.32 = f32[4,128,128]{1,2,0:T(8,128)S(1)} custom-call(f32[4,128,128]{2,1,0:T(8,128)S(1)} %get-tuple-element.18), custom_call_target="InvertDiagBlocksLowerTriangular" | custom-call | tf_op jit(solution)/shard_map/jit(_cho_solve)/triangular_solve | solution.py:26
  574.2 2.1 fusion.65
  576.3 2.0 convolution_subtract_fusion.9
  579.3 2.0 convolution_subtract_fusion.5
  582.3 2.8 fusion.35
  591.2 1.8 fusion.32
  593.0 1.8 fusion.108
  596.9 2.0 pad_maximum_fusion.1
  598.9 263.6 %all-reduce.8.cloned.1.call-done = f32[512,1512]{0,1:T(8,128)} async-done(((f32[512,1512]{0,1:T(8,128)}), f32[512,1512]{0,1:T(8,128)}) %all-reduce.8.cloned.1.call-update) | async-done | bytes 3096592 | tf_op jit(solution)/shard_map/psum | solution.py:59
  862.5 2.3 select_add_fusion.1
  864.8 1.6 copy.9
  866.4 1.5 fusion.44
  868.8 11.7 %cholesky.358 = f32[128,128]{1,0:T(8,128)S(1)} custom-call(f32[128,128]{1,0:T(8,128)S(1)} %cholesky.439), custom_call_target="Cholesky" | custom-call | tf_op jit(solution)/shard_map/jit(cholesky)/cholesky | solution.py:25
  880.7 9.8 custom-call.33
  893.7 13.3 %cholesky.377 = f32[128,128]{1,0:T(8,128)} custom-call(f32[128,128]{1,0:T(8,128)} %cholesky.443), custom_call_target="Cholesky" | custom-call | tf_op jit(solution)/shard_map/jit(cholesky)/cholesky | solution.py:25
  907.0 1.5 select_reduce_fusion.2
  909.9 11.3 %custom-call.34 = f32[1,128,128]{1,2,0:T(8,128)} custom-call(f32[1,128,128]{2,1,0:T(8,128)} %get-tuple-element.50), custom_call_target="InvertDiagBlocksLowerTriangular" | custom-call | tf_op jit(solution)/shard_map/jit(cholesky)/cholesky | solution.py:25
  923.6 12.3 %cholesky.398 = f32[128,128]{1,0:T(8,128)} custom-call(f32[128,128]{1,0:T(8,128)S(1)} %cholesky.448), custom_call_target="Cholesky" | custom-call | tf_op jit(solution)/shard_map/jit(cholesky)/cholesky | solution.py:25
  937.4 10.6 %custom-call.35 = f32[1,128,128]{1,2,0:T(8,128)} custom-call(f32[1,128,128]{2,1,0:T(8,128)S(1)} %get-tuple-element.47), custom_call_target="InvertDiagBlocksLowerTriangular" | custom-call | tf_op jit(solution)/shard_map/jit(cholesky)/cholesky | solution.py:25
  950.3 11.7 %cholesky.415 = f32[128,128]{1,0:T(8,128)S(1)} custom-call(f32[128,128]{1,0:T(8,128)S(1)} %convolution_subtract_fusion.14), custom_call_target="Cholesky" | custom-call | tf_op jit(solution)/shard_map/jit(cholesky)/cholesky | solution.py:25
  967.2 14.0 %while.5 = (s32[]{:T(128)}, f32[512,512]{1,0:T(8,128)}, s32[4,2]{0,1:T(2,128)S(1)}, f32[4,128,128]{2,1,0:T(8,128)}, s32[]{:T(128)}) while((s32[]{:T(128)}, f32[512,512]{1,0:T(8,128)}, s32[4,2]{0,1:T(2,128)S(1)}, f32[4,128,128]{2,1,0:T(8,128)}, s32[]{:T(128)}) %tuple.70), condition=%wide.while_cond.clone, body=%wide.while_body.clone.sunk | while | flops 2 | bytes 132705 | solution.py:26
  967.8 2.9 bitcast_dynamic-update-slice_fusion.5
  971.3 2.9 bitcast_dynamic-update-slice_fusion.5
  974.8 2.9 bitcast_dynamic-update-slice_fusion.5
  978.3 2.8 bitcast_dynamic-update-slice_fusion.5
  981.2 40.2 %custom-call.36 = f32[4,128,128]{1,2,0:T(8,128)S(1)} custom-call(f32[4,128,128]{2,1,0:T(8,128)} %get-tuple-element.19), custom_call_target="InvertDiagBlocksLowerTriangular" | custom-call | tf_op jit(solution)/shard_map/jit(_cho_solve)/triangular_solve | solution.py:26
  1021.4 2.0 fusion.63
  1023.4 2.1 convolution_subtract_fusion.7
  1026.4 2.0 convolution_subtract_fusion.3
  1029.4 2.8 fusion.29
  1038.2 1.8 fusion.26
  1042.7 1.8 select_add_fusion
  (119 shorter events, 56.1 us)
Async XLA Ops:
  7.2 161.5 %all-reduce.10.cloned.1.call-start = ((), (), s32[]{:S(2)}) async-start(), calls=%async_computation.2 | async-start | bytes 4194304 | tf_op jit(solution)/shard_map/psum | solution.py:9
  11.3 3.2 copy-start.9
  14.4 156.3 %copy-start.7 = (bf16[192,1000]{1,0:T(8,128)(2,1)S(1)}, bf16[192,1000]{1,0:T(8,128)(2,1)}, u32[]{:S(2)}) copy-start(bf16[192,1000]{1,0:T(8,128)(2,1)} %param.11) | copy-start | bytes 1152004
  14.5 156.3 %copy-start.10 = (s32[192]{0:T(256)S(1)}, s32[192]{0:T(256)}, u32[]{:S(2)}) copy-start(s32[192]{0:T(256)} %param.10) | copy-start | bytes 2308
  14.5 424.7 %all-reduce.6.cloned.1.call-start = ((), (), s32[]{:S(2)}) async-start(), calls=%async_computation | async-start | bytes 6193152 | tf_op jit(solution)/shard_map/psum | solution.py:59
  173.4 1.2 copy-start.11
  173.4 689.1 %all-reduce.8.cloned.1.call-start = ((), (), s32[]{:S(2)}) async-start(), calls=%async_computation.1 | async-start | bytes 6193152 | tf_op jit(solution)/shard_map/psum | solution.py:59
  574.2 15.6 %copy-start.4 = (f32[4,128,128]{1,2,0:T(8,128)}, f32[4,128,128]{1,2,0:T(8,128)S(1)}, u32[]{:S(2)}) copy-start(f32[4,128,128]{1,2,0:T(8,128)S(1)} %custom-call.32) | copy-start | bytes 786436
  591.2 3.7 copy-start.8
  595.4 3.5 copy-start.5
  595.4 1.5 copy-start.1
  867.8 1.0 copy-start.2
  981.2 45.2 %copy-start = (f32[512,512]{1,0:T(8,128)S(1)}, f32[512,512]{1,0:T(8,128)}, u32[]{:S(2)}) copy-start(f32[512,512]{1,0:T(8,128)} %get-tuple-element.172) | copy-start | bytes 3145732
  1038.2 2.8 copy-start.6
  1041.0 1.7 copy-start.3
Sparse Core Ops, SparseCore 0:
  14.6 154.0 all-reduce.9
  175.0 264.0 all-reduce.5
  599.0 263.4 all-reduce.7
where the time goes:
time: 1060 us; the launch traced here: 1050 us
  waiting for transfers between devices  680 us (64%)
  other arithmetic  263 us (25%)
  matrix products  55.9 us (5%)
  local copies, waits for them, and re-layouts  30.6 us (3%)
  between operations  21.4 us (2%)
    psum x2, waiting for transfers between devices, shards(): summed = lax.psum(stacked, ('rows', 'rrep'))  526 us
    another operation x29, other arithmetic, ridge_solve(): cholesky_factor = jnp.linalg.cholesky(gram + ridge)  165 us
    psum x1, waiting for transfers between devices, spread(): return lax.psum(jnp.where(mine, value, jnp.zeros_like(value)), axis)  154 us
    another operation x5, other arithmetic, ridge_solve(): return jax.scipy.linalg.cho_solve((cholesky_factor, True), product)  80.8 us
    another operation x28, matrix products, ridge_solve(): return jax.scipy.linalg.cho_solve((cholesky_factor, True), product)  40 us
    another operation x27, local copies, waits for them, and re-layouts, ridge_solve(): return jax.scipy.linalg.cho_solve((cholesky_factor, True), product)  23.2 us
  transfers between devices with their start and end apart: 3, of which 3 were waited for; matrix products, arithmetic and copies ran while one was open for 0% of the time, Pallas kernels for 0%

commit v1 on v0

v1 whole, which is shorter than its diff:
```python
import functools

import jax
import jax.numpy as jnp
from jax import lax
from jax.experimental import pallas as pl
from jax.experimental.pallas import tpu as pltpu
from jax.sharding import PartitionSpec as P

MESH = pl.DeviceIdType.MESH
HI = lax.Precision.HIGHEST
F32 = jnp.float32
BF16 = jnp.bfloat16
NX, NY, NZ = 4, 4, 8
BLOCK = 512
CLASSES = 1024
VMEM_LIMIT = 48 * 2**20


class Place:
    def __init__(self):
        rows, rrep = lax.axis_index("rows"), lax.axis_index("rrep")
        self.rows, self.rrep = rows, rrep
        self.y, self.z = rows // NZ, rows % NZ
        self.x, self.c = rrep // 2, rrep % 2

    def at_x(self, d):
        other = (self.x + d) % NX
        return other, (self.rows, other * 2 + self.c)

    def at_y(self, d):
        other = (self.y + d) % NY
        return other, (other * NZ + self.z, self.rrep)

    def at_z(self, d):
        other = (self.z + d) % NZ
        return other, (self.y * NZ + other, self.rrep)

    def partner(self):
        return (self.rows, self.x * 2 + 1 - self.c)

    def greet(self, axes):
        barrier = pltpu.get_barrier_semaphore()
        peers = []
        if "x" in axes:
            peers += [self.at_x(d)[1] for d in range(1, NX)]
        if "y" in axes:
            peers += [self.at_y(d)[1] for d in range(1, NY)]
        if "z" in axes:
            peers += [self.at_z(d)[1] for d in range(1, NZ)]
        if "c" in axes:
            peers += [self.partner()]
        for peer in peers:
            pl.semaphore_signal(barrier, inc=1, device_id=peer, device_id_type=MESH)
        pl.semaphore_wait(barrier, len(peers))


class Sender:
    def __init__(self, send_sems, recv_sems):
        self.send_sems, self.recv_sems = send_sems, recv_sems
        self.copies = []

    def start(self, src, dst, device):
        i = len(self.copies)
        copy = pltpu.make_async_remote_copy(
            src_ref=src,
            dst_ref=dst,
            send_sem=self.send_sems.at[i],
            recv_sem=self.recv_sems.at[i],
            device_id=device,
            device_id_type=MESH,
        )
        copy.start()
        self.copies.append(copy)
        return copy

    def drain(self):
        for copy in self.copies:
            copy.wait_send()


def arrive(copies):
    for copy in copies:
        copy.wait_recv()


LAND_COPIES = 2 + 3 + 7 + 7 + 6 + 6 + 1


def land_kernel(zin, xin, rin, zout, xp, rp, r1, s1, r2, send_sems, recv_sems):
    me = Place()
    me.greet("xyzc")
    out = Sender(send_sems, recv_sems)
    x, y, z, c = me.x, me.y, me.z, me.c
    first = []
    for d in range(1, NY):
        other, device = me.at_y(d)
        first.append(out.start(zin.at[other], r1.at[d - 1], device))
    swap = [out.start(xin, xp, me.partner()), out.start(rin, rp, me.partner())]
    arrive(first)
    s1[...] = zin[y] + r1[0] + r1[1] + r1[2]
    second = []
    for d in range(1, NZ):
        other, device = me.at_z(d)
        second.append(out.start(s1.at[other], r2.at[d - 1], device))
    arrive(second)
    total = s1[z]
    for d in range(1, NZ):
        total = total + r2[d - 1]
    s, g = z // 4, z % 4
    zout[y, s, x, c, g] = total
    third = []
    for d in range(1, NZ):
        _, device = me.at_z(d)
        third.append(out.start(zout.at[y, s, x, c, g], zout.at[y, s, x, c, g], device))
    arrive(third)
    fourth = []
    for d in range(1, 4):
        fourth.append(out.start(zout.at[y, 0, x, c], zout.at[y, 0, x, c], me.at_y(d)[1]))
        fourth.append(out.start(zout.at[y, 1, x, c], zout.at[y, 1, x, c], me.at_x(d)[1]))
    arrive(fourth)
    fifth = []
    for d in range(1, 4):
        fifth.append(out.start(zout.at[:, 0, x, c], zout.at[:, 0, x, c], me.at_x(d)[1]))
        fifth.append(out.start(zout.at[y, 1, :, c], zout.at[y, 1, :, c], me.at_y(d)[1]))
    arrive(fifth)
    last = out.start(zout.at[:, :, :, c], zout.at[:, :, :, c], me.partner())
    arrive([last])
    arrive(swap)
    out.drain()


def land(zin, xhat, rounded):
    rows = xhat.shape[0]
    vmem = pl.BlockSpec(memory_space=pltpu.VMEM)
    return pl.pallas_call(
        land_kernel,
        out_shape=(
            jax.ShapeDtypeStruct((NY, 2, NX, 2, 4, 16, 256), BF16),
            jax.ShapeDtypeStruct((rows, 1024), BF16),
            jax.ShapeDtypeStruct((rows, CLASSES), BF16),
        ),
        in_specs=[vmem] * 3,
        out_specs=(vmem,) * 3,
        scratch_shapes=[
            pltpu.VMEM((NY - 1, NZ, 16, 256), BF16),
            pltpu.VMEM((NZ, 16, 256), BF16),
            pltpu.VMEM((NZ - 1, 16, 256), BF16),
            pltpu.SemaphoreType.DMA((LAND_COPIES,)),
            pltpu.SemaphoreType.DMA((LAND_COPIES,)),
        ],
        compiler_params=pltpu.CompilerParams(
            collective_id=0, has_side_effects=True, vmem_limit_bytes=VMEM_LIMIT
        ),
        name="land",
    )(zin, xhat, rounded)


def partial_kernel(zall, xo, xp, ro, rp, kout, gout, pout, kern, resid):
    rows = xo.shape[0]
    c = lax.axis_index("rrep") % 2
    for half, xref in enumerate((xo, xp)):
        total = None
        for y in range(NY):
            zy = zall[y].reshape(2 * BLOCK, 256)
            part = lax.dot_general(
                xref[:, y * 256 : (y + 1) * 256],
                zy,
                (((1,), (1,)), ((), ())),
                preferred_element_type=F32,
            )
            total = part if total is None else total + part
        kern[half * rows : (half + 1) * rows, :] = jnp.exp(total * (1024**-0.5)).astype(BF16)
    kout[...] = kern[:rows, :]
    resid[:rows, :] = ro[...]
    resid[rows:, :] = rp[...]
    contract = (((0,), (0,)), ((), ()))
    mine = kern[:, pl.ds(pl.multiple_of(c * BLOCK, BLOCK), BLOCK)]
    cross = kern[:, pl.ds(pl.multiple_of(BLOCK + c * 256, 256), 256)]
    for y in range(NY):
        cols = kern[:, pl.ds(pl.multiple_of(c * BLOCK + y * 128, 128), 128)]
        first = kern[:, y * 128 : (y + 1) * 128]
        gram = lax.dot_general(mine, cols, contract, preferred_element_type=F32)
        side = lax.dot_general(cross, first, contract, preferred_element_type=F32)
        both = jnp.concatenate([gram, side], axis=0)
        for x in range(NX):
            gout[x, y] = both[x * 192 : (x + 1) * 192].reshape(NZ, 24, 128)
    for k in range(4):
        prod = lax.dot_general(
            resid[:, k * 256 : (k + 1) * 256], mine, contract, preferred_element_type=F32
        )
        pout[k] = prod.astype(BF16).reshape(NY, 64, BLOCK)


def partials(zall, xo, xp, ro, rp):
    rows = xo.shape[0]
    vmem = pl.BlockSpec(memory_space=pltpu.VMEM)
    return pl.pallas_call(
        partial_kernel,
        out_shape=(
            jax.ShapeDtypeStruct((rows, 2 * BLOCK), BF16),
            jax.ShapeDtypeStruct((NX, NY, NZ, 24, 128), F32),
            jax.ShapeDtypeStruct((NX, NY, 64, BLOCK), BF16),
        ),
        in_specs=[vmem] * 5,
        out_specs=(vmem,) * 3,
        scratch_shapes=[
            pltpu.VMEM((2 * rows, 2 * BLOCK), BF16),
            pltpu.VMEM((2 * rows, CLASSES), BF16),
        ],
        compiler_params=pltpu.CompilerParams(vmem_limit_bytes=VMEM_LIMIT),
        name="partials",
    )(zall, xo, xp, ro, rp)


SUM_COPIES = 12 + 12 + 14 + 7 + 6 + 6


def sum_kernel(
    gin, pin, gout, pout, ra, rb, qa, qb, ga, gb, pa, pb, ra2, rb2, qa2, qb2, g2, p2, r3, q3, send_sems, recv_sems
):
    me = Place()
    me.greet("xyz")
    out = Sender(send_sems, recv_sems)
    x, y, z = me.x, me.y, me.z
    copies = []
    for d in range(1, 4):
        i, device = me.at_x(d)
        copies.append(out.start(gin.at[i, :, 0:4], ra.at[d - 1], device))
        copies.append(out.start(pin.at[i, :, 0:32], qa.at[d - 1], device))
        i, device = me.at_y(d)
        copies.append(out.start(gin.at[:, i, 4:8], rb.at[d - 1], device))
        copies.append(out.start(pin.at[:, i, 32:64], qb.at[d - 1], device))
    arrive(copies)
    ga[...] = gin[x, :, 0:4] + ra[0] + ra[1] + ra[2]
    gb[...] = gin[:, y, 4:8] + rb[0] + rb[1] + rb[2]
    wide = lambda value: value.astype(F32)
    pa[...] = (wide(pin[x, :, 0:32]) + wide(qa[0]) + wide(qa[1]) + wide(qa[2])).astype(BF16)
    pb[...] = (wide(pin[:, y, 32:64]) + wide(qb[0]) + wide(qb[1]) + wide(qb[2])).astype(BF16)
    copies = []
    for d in range(1, 4):
        i, device = me.at_y(d)
        copies.append(out.start(ga.at[i], ra2.at[d - 1], device))
        copies.append(out.start(pa.at[i], qa2.at[d - 1], device))
        i, device = me.at_x(d)
        copies.append(out.start(gb.at[i], rb2.at[d - 1], device))
        copies.append(out.start(pb.at[i], qb2.at[d - 1], device))
    arrive(copies)
    g2[0:4] = ga[y] + ra2[0] + ra2[1] + ra2[2]
    g2[4:8] = gb[x] + rb2[0] + rb2[1] + rb2[2]
    sa = wide(pa[y]) + wide(qa2[0]) + wide(qa2[1]) + wide(qa2[2])
    sb = wide(pb[x]) + wide(qb2[0]) + wide(qb2[1]) + wide(qb2[2])
    p2[0:4] = sa.reshape(4, 8, BLOCK)
    p2[4:8] = sb.reshape(4, 8, BLOCK)
    copies = []
    for d in range(1, NZ):
        i, device = me.at_z(d)
        copies.append(out.start(g2.at[i], r3.at[d - 1], device))
        copies.append(out.start(p2.at[i], q3.at[d - 1], device))
    arrive(copies)
    gram, prod = g2[z], p2[z]
    for d in range(1, NZ):
        gram = gram + r3[d - 1]
        prod = prod + q3[d - 1]
    gout[x, y, z] = gram
    pout[...] = prod
    copies = []
    for d in range(1, NZ):
        copies.append(out.start(gout.at[x, y, z], gout.at[x, y, z], me.at_z(d)[1]))
    arrive(copies)
    copies = []
    for d in range(1, 4):
        copies.append(out.start(gout.at[x, y, 0:4], gout.at[x, y, 0:4], me.at_y(d)[1]))
        copies.append(out.start(gout.at[x, y, 4:8], gout.at[x, y, 4:8], me.at_x(d)[1]))
    arrive(copies)
    copies = []
    for d in range(1, 4):
        copies.append(out.start(gout.at[x, :, 0:4], gout.at[x, :, 0:4], me.at_x(d)[1]))
        copies.append(out.start(gout.at[:, y, 4:8], gout.at[:, y, 4:8], me.at_y(d)[1]))
    arrive(copies)
    out.drain()


def sums(gram, prod):
    vmem = pl.BlockSpec(memory_space=pltpu.VMEM)
    return pl.pallas_call(
        sum_kernel,
        out_shape=(
            jax.ShapeDtypeStruct((NX, NY, NZ, 24, 128), F32),
            jax.ShapeDtypeStruct((8, BLOCK), F32),
        ),
        in_specs=[vmem] * 2,
        out_specs=(vmem,) * 2,
        scratch_shapes=[
            pltpu.VMEM((3, 4, 4, 24, 128), F32),
            pltpu.VMEM((3, 4, 4, 24, 128), F32),
            pltpu.VMEM((3, 4, 32, BLOCK), BF16),
            pltpu.VMEM((3, 4, 32, BLOCK), BF16),
            pltpu.VMEM((4, 4, 24, 128), F32),
            pltpu.VMEM((4, 4, 24, 128), F32),
            pltpu.VMEM((4, 32, BLOCK), BF16),
            pltpu.VMEM((4, 32, BLOCK), BF16),
            pltpu.VMEM((3, 4, 24, 128), F32),
            pltpu.VMEM((3, 4, 24, 128), F32),
            pltpu.VMEM((3, 32, BLOCK), BF16),
            pltpu.VMEM((3, 32, BLOCK), BF16),
            pltpu.VMEM((NZ, 24, 128), F32),
            pltpu.VMEM((NZ, 8, BLOCK), F32),
            pltpu.VMEM((NZ - 1, 24, 128), F32),
            pltpu.VMEM((NZ - 1, 8, BLOCK), F32),
            pltpu.SemaphoreType.DMA((SUM_COPIES,)),
            pltpu.SemaphoreType.DMA((SUM_COPIES,)),
        ],
        compiler_params=pltpu.CompilerParams(
            collective_id=1, has_side_effects=True, vmem_limit_bytes=VMEM_LIMIT
        ),
        name="sums",
    )(gram, prod)


def eliminate_rows(values, k, n):
    lane = lax.broadcasted_iota(jnp.int32, (8, n), 1)
    sub = lax.broadcasted_iota(jnp.int32, (8, n), 0)
    rows = values[k : k + 8, :]
    pivots = [jnp.broadcast_to(rows[:, k + q : k + q + 1], (8, n)) for q in range(8)]
    inside = (lane >= k) & (lane < k + 8)
    panel = jnp.where(inside, (lane - k == sub).astype(F32), rows)
    for q in range(8):
        factor = pivots[q]
        inverse = 1.0 / jnp.broadcast_to(factor[q : q + 1, :], (8, n))
        own = sub == q

        def update(block):
            row = jnp.broadcast_to(block[q : q + 1, :], (8, n)) * inverse
            return jnp.where(own, row, block - factor * row)

        for j in range(q + 1, 8):
            pivots[j] = update(pivots[j])
        panel = update(panel)
    return panel


def invert_tile(values, n):
    lane = lax.broadcasted_iota(jnp.int32, (n, n), 1)
    for k in range(0, n, 8):
        panel = eliminate_rows(values, k, n)
        inside = (lane >= k) & (lane < k + 8)
        rest = jnp.where(inside, 0.0, values)
        for q in range(8):
            column = jnp.broadcast_to(values[:, k + q : k + q + 1], (n, n))
            rest = rest - column * jnp.broadcast_to(panel[q : q + 1, :], (n, n))
        parts = ([rest[:k]] if k else []) + [panel] + ([rest[k + 8 :]] if k + 8 < n else [])
        values = jnp.concatenate(parts, axis=0)
    return values


def invert(ref, n, tiles):
    b = n // tiles
    for j in range(tiles):
        s = slice(j * b, (j + 1) * b)
        inverse = invert_tile(ref[s, s], b)
        row = jnp.dot(inverse, ref[s, :], precision=HI, preferred_element_type=F32)
        column = ref[:, s]
        ref[:, s] = jnp.zeros((n, b), F32)
        parts = ([row[:, : j * b]] if j else []) + [inverse]
        parts += [row[:, (j + 1) * b :]] if j < tiles - 1 else []
        row = jnp.concatenate(parts, axis=1)
        for i in range(tiles):
            t = slice(i * b, (i + 1) * b)
            if i != j:
                ref[t, :] -= jnp.dot(column[t], row, precision=HI, preferred_element_type=F32)
        ref[s, :] = row


def solve_kernel(ridge, gram, prod, inv, side, delta, part, full):
    for x in range(NX):
        for y in range(NY):
            full[x * 192 : (x + 1) * 192, y * 128 : (y + 1) * 128] = gram[x, y].reshape(192, 128)
    rows = lax.broadcasted_iota(jnp.int32, (BLOCK, BLOCK), 0)
    cols = lax.broadcasted_iota(jnp.int32, (BLOCK, BLOCK), 1)
    inv[...] = full[:BLOCK] + jnp.where(rows == cols, ridge, 0.0)
    side[...] = full[BLOCK:]
    invert(inv, BLOCK, 4)
    first = jnp.dot(prod[...], inv[...], precision=HI, preferred_element_type=F32)
    delta[...] = first
    part[...] = across(first, side[...])


def across(delta, side):
    return lax.dot_general(
        delta.astype(BF16).astype(F32),
        side,
        (((1,), (1,)), ((), ())),
        precision=HI,
        preferred_element_type=F32,
    )


def solve(gram, prod, ridge):
    vmem = pl.BlockSpec(memory_space=pltpu.VMEM)
    return pl.pallas_call(
        functools.partial(solve_kernel, ridge),
        out_shape=(
            jax.ShapeDtypeStruct((BLOCK, BLOCK), F32),
            jax.ShapeDtypeStruct((256, BLOCK), F32),
            jax.ShapeDtypeStruct((8, BLOCK), F32),
            jax.ShapeDtypeStruct((8, 256), F32),
        ),
        in_specs=[vmem] * 2,
        out_specs=(vmem,) * 4,
        scratch_shapes=[pltpu.VMEM((768, BLOCK), F32)],
        compiler_params=pltpu.CompilerParams(vmem_limit_bytes=VMEM_LIMIT),
        name="solve",
    )(gram, prod)


SPREAD_COPIES = 2 + 7 + 6 + 6 + 1


def spread_kernel(inv, side, prod, delta, part, dout, other, opart, dz, send_sems, recv_sems):
    me = Place()
    me.greet("xyzc")
    out = Sender(send_sems, recv_sems)
    x, y, z, c = me.x, me.y, me.z, me.c
    copies = [out.start(delta, other, me.partner()), out.start(part, opart, me.partner())]
    arrive(copies)
    cross = jnp.concatenate([opart[...], across(other[...], side[...])], axis=1)
    second = jnp.dot(prod[...] - cross, inv[...], precision=HI, preferred_element_type=F32)
    dz[z] = jnp.where(c == 0, delta[...], second)
    copies = []
    for d in range(1, NZ):
        copies.append(out.start(dz.at[z], dz.at[z], me.at_z(d)[1]))
    arrive(copies)
    dout[c, x, y] = dz[...].reshape(64, BLOCK).astype(BF16)
    copies = []
    for d in range(1, 4):
        copies.append(out.start(dout.at[c, x, y, 0:32], dout.at[c, x, y, 0:32], me.at_y(d)[1]))
        copies.append(out.start(dout.at[c, x, y, 32:64], dout.at[c, x, y, 32:64], me.at_x(d)[1]))
    arrive(copies)
    copies = []
    for d in range(1, 4):
        copies.append(out.start(dout.at[c, x, :, 0:32], dout.at[c, x, :, 0:32], me.at_x(d)[1]))
        copies.append(out.start(dout.at[c, :, y, 32:64], dout.at[c, :, y, 32:64], me.at_y(d)[1]))
    arrive(copies)
    arrive([out.start(dout.at[c], dout.at[c], me.partner())])
    out.drain()


def spread(inv, side, prod, delta, part):
    vmem = pl.BlockSpec(memory_space=pltpu.VMEM)
    return pl.pallas_call(
        spread_kernel,
        out_shape=jax.ShapeDtypeStruct((2, NX, NY, 64, BLOCK), BF16),
        in_specs=[vmem] * 5,
        out_specs=vmem,
        scratch_shapes=[
            pltpu.VMEM((8, BLOCK), F32),
            pltpu.VMEM((8, 256), F32),
            pltpu.VMEM((NZ, 8, BLOCK), F32),
            pltpu.SemaphoreType.DMA((SPREAD_COPIES,)),
            pltpu.SemaphoreType.DMA((SPREAD_COPIES,)),
        ],
        compiler_params=pltpu.CompilerParams(
            collective_id=2, has_side_effects=True, vmem_limit_bytes=VMEM_LIMIT
        ),
        name="spread",
    )(inv, side, prod, delta, part)


def unit_normalize(values):
    wide = values.astype(F32)
    scale = lax.rsqrt(jnp.mean(wide * wide, axis=1, keepdims=True) + 1e-06)
    return (wide * scale).astype(BF16)


def shards(features, labels, scores, landmarks, coefficients, block_ids):
    count = coefficients.shape[1]
    devices_all = lax.axis_size("rows") * lax.axis_size("rrep")
    ridge = float(features.shape[0] * devices_all)
    holder = lax.axis_index("rows")
    replica = lax.axis_index("rrep")
    xhat = unit_normalize(features)
    classes = jnp.arange(count, dtype=jnp.int32)
    residual = (labels[:, None] == classes[None, :]).astype(F32) - scores.astype(F32)
    rounded = jnp.pad(residual.astype(BF16), ((0, 0), (0, CLASSES - count)))
    share = landmarks.shape[0] // 8
    zslice = unit_normalize(lax.dynamic_slice_in_dim(landmarks, replica * share, share, 0))
    mine = (block_ids == holder)[:, None, None]
    zin = jnp.where(mine, zslice[None], jnp.zeros_like(zslice)[None])
    zin = zin.reshape(2, 4, 16, NY, 256).transpose(3, 0, 1, 2, 4).reshape(NY, NZ, 16, 256)
    zall, xp, rp = land(zin, xhat, rounded)
    kern, gram, prod = partials(zall, xhat, xp, rounded, rp)
    gram, prod = sums(gram, prod)
    inv, side, delta, part = solve(gram, prod, ridge)
    deltas = spread(inv, side, prod, delta, part).reshape(2, CLASSES, BLOCK)[:, :count]
    new_coefficients = coefficients
    for step in range(2):
        added = jnp.where(holder == block_ids[step], deltas[step].T.astype(F32), 0.0)
        new_coefficients = new_coefficients + added
        residual = residual - lax.dot_general(
            kern[:, step * BLOCK : (step + 1) * BLOCK],
            deltas[step],
            (((1,), (1,)), ((), ())),
            preferred_element_type=F32,
        )
    return (new_coefficients, residual)


def solution(mesh):
    in_specs = (
        P(("rows", "rrep"), None),
        P(("rows", "rrep")),
        P(("rows", "rrep"), None),
        P("rows", None),
        P("rows", None),
        P(),
    )
    out_specs = (P("rows", None), P(("rows", "rrep"), None))
    return jax.shard_map(shards, mesh=mesh, in_specs=in_specs, out_specs=out_specs, check_vma=False)
```

time: 1060 us -> 158 us (0.15)
  waiting for transfers between devices: 680 us -> 0 us
  other arithmetic: 263 us -> 7.39 us
  Pallas kernels: 0 us -> 144 us
  matrix products: 55.9 us -> 1.87 us
  local copies, waits for them, and re-layouts: 30.6 us -> 2.24 us
  between operations: 21.4 us -> 2.07 us
    psum x3 -> x0, waiting for transfers between devices: 680 us -> none  [the longest x2 526 us: shards(): summed = lax.psum(stacked, ('rows', 'rrep'))]
    another operation x34 -> x0, other arithmetic: 246 us -> none  [the longest x29 165 us: ridge_solve(): cholesky_factor = jnp.linalg.cholesky(gram + ridge)]
    pallas_call x0 -> x5, Pallas kernels: none -> 144 us  [the longest x1 48 us: sums(): pl.pallas_call(sum_kernel, out_shape=(jax.ShapeDtypeStruct((NX, NY, NZ, 2...]
    another operation x40 -> x0, matrix products: 49 us -> none  [the longest x28 40 us: ridge_solve(): return jax.scipy.linalg.cho_solve((cholesky_factor, True), product)]
    another operation x35 -> x0, local copies, waits for them, and re-layouts: 24.1 us -> none  [the longest x27 23.2 us: ridge_solve(): return jax.scipy.linalg.cho_solve((cholesky_factor, True), product)]
  transfers between devices with their start and end apart: 3 -> 0, of which waited for: 3 -> 0; matrix products, arithmetic and copies ran while one was open for 0% -> 0% of each run, Pallas kernels for 0% -> 0%
where the time goes in v1:
time: 158 us
  Pallas kernels  144 us (91%)
  other arithmetic  7.39 us (5%)
  local copies, waits for them, and re-layouts  2.24 us (1%)
  between operations  2.07 us (1%)
  matrix products  1.87 us (1%)
    pallas_call x1, Pallas kernels, sums(): pl.pallas_call(sum_kernel, out_shape=(jax.ShapeDtypeStruct((NX, NY, NZ, 2...  48 us
    pallas_call x1, Pallas kernels, land(): pl.pallas_call(land_kernel, out_shape=(jax.ShapeDtypeStruct((NY, 2, NX, 2...  39.9 us
    pallas_call x1, Pallas kernels, spread(): pl.pallas_call(spread_kernel, out_shape=jax.ShapeDtypeStruct((2, NX, NY,...  31.8 us
    pallas_call x1, Pallas kernels, solve(): pl.pallas_call(functools.partial(solve_kernel, ridge), out_shape=(jax.Sha...  19.6 us
    pallas_call x1, Pallas kernels, partials(): pl.pallas_call(partial_kernel, out_shape=(jax.ShapeDtypeStruct((rows, 2 *...  4.55 us
    add x1, other arithmetic, shards(): new_coefficients = new_coefficients + added  3.33 us

profile of v1, /device:TPU:1, one launch (start us, length us, event | category | flops | bytes accessed | tf_op | source)
XLA Modules:
  0.0 157.5 jit_solution(11024515777512374732)
XLA Ops:
  0.6 0.0 copy-start.2
  0.6 0.0 copy-start.1
  0.7 1.1 fusion.3
  1.8 1.0 fusion.4
  2.8 0.1 broadcast_in_dim.48
  2.9 0.7 broadcast_compare_fusion
  3.6 0.1 broadcast_in_dim.45
  3.7 0.1 broadcast_in_dim.46
  3.7 0.1 broadcast_select_fusion.zin
  3.8 0.0 copy-done.2
  3.8 0.9 fusion.2
  4.8 0.0 copy-done.1
  4.8 0.2 fusion
  5.0 0.1 fusion.1.xin.xo
  5.1 39.9 %land.1 = (bf16[4,2,4,2,4,16,256]{6,5,4,3,2,1,0:T(8,128)(2,1)S(1)}, bf16[192,1024]{1,0:T(8,128)(2,1)S(1)}, bf16[192,1024]{1,0:T(8,128)(2,1)S(1)}) custom-call(bf16[4,8,16,256]{3,2,1,0:T(8,128)(2,1)S(1)} %broadcast_select_fusion.zin, bf16[192,1024]{1,0:T(8,128)(2,1)S(1)} %fusion.1.xin.xo, bf16[192,1024]{1,0:T(8,128)(2,1)S(1)} %pad.4.rin.ro), custom_call_target="tpu_custom_call" | custom-call | tf_op jit(solution)/shard_map/land/pallas_call | solution.py:136
  45.1 0.0 copy-start
  45.1 1.3 copy-done
  46.4 4.5 %partials.1 = (bf16[192,1024]{1,0:T(8,128)(2,1)S(1)}, f32[4,4,8,24,128]{4,3,2,1,0:T(8,128)S(1)}, bf16[4,4,64,512]{3,2,1,0:T(8,128)(2,1)S(1)}) custom-call(bf16[4,2,4,2,4,16,256]{6,5,4,3,2,1,0:T(8,128)(2,1)} %copy-done, bf16[192,1024]{1,0:T(8,128)(2,1)S(1)} %fusion.1.xin.xo, bf16[192,1024]{1,0:T(8,128)(2,1)S(1)} %get-tuple-element.15.xp, ...), custom_call_target="tpu_custom_call" | custom-call | tf_op jit(solution)/shard_map/partials/pallas_call | solution.py:198
  50.9 48.0 %sums.1 = (f32[4,4,8,24,128]{4,3,2,1,0:T(8,128)S(1)}, f32[8,512]{1,0:T(8,128)S(1)}) custom-call(f32[4,4,8,24,128]{4,3,2,1,0:T(8,128)S(1)} %get-tuple-element.17.gin, bf16[4,4,64,512]{3,2,1,0:T(8,128)(2,1)S(1)} %get-tuple-element.18.pin), custom_call_target="tpu_custom_call" | custom-call | tf_op jit(solution)/shard_map/sums/pallas_call | solution.py:286
  98.9 19.6 %solve.1 = (f32[512,512]{1,0:T(8,128)S(1)}, f32[256,512]{1,0:T(8,128)S(1)}, f32[8,512]{1,0:T(8,128)S(1)}, f32[8,256]{1,0:T(8,128)S(1)}) custom-call(f32[4,4,8,24,128]{4,3,2,1,0:T(8,128)S(1)} %get-tuple-element.19.gram, f32[8,512]{1,0:T(8,128)S(1)} %get-tuple-element.20.prod), custom_call_target="tpu_custom_call" | custom-call | tf_op jit(solution)/shard_map/solve/pallas_call | solution.py:401
  118.6 0.0 copy-start.4
  118.6 31.8 %spread.1 = bf16[2,4,4,64,512]{4,3,2,1,0:T(8,128)(2,1)S(1)} custom-call(f32[512,512]{1,0:T(8,128)S(1)} %get-tuple-element.21.inv, f32[256,512]{1,0:T(8,128)S(1)} %get-tuple-element.22.side, f32[8,512]{1,0:T(8,128)S(1)} %get-tuple-element.20.prod, f32[8,512]{1,0:T(8,128)S(1)} %get-tuple-element.23.delta, f32[8,256]{1,0:T(8,128)S(1)} %get-tuple-element.24.part), custom_call_target="tpu_custom_call" | custom-call | tf_op jit(solution)/shard_map/spread/pallas_call | solution.py:451
  150.4 0.0 copy-done.4
  150.4 0.0 copy-start.3
  150.5 0.5 convolution_subtract_fusion.1
  151.0 1.4 convolution_subtract_fusion
  152.3 0.0 copy-done.3
  152.3 0.6 fusion.7
  154.2 3.3 %bitcast_add_fusion = f32[512,1000]{0,1:T(8,128)} fusion(f32[512,1000]{0,1:T(8,128)} %param.10, pred[]{:T(512)S(6)} %eq.31, pred[]{:T(512)S(6)} %eq.25, bf16[2,1024,512]{2,1,0:T(8,128)(2,1)S(1)} %bitcast.23), kind=kLoop, calls=%fused_computation | loop fusion | flops 3072000 | bytes 6144002 | tf_op jit(solution)/shard_map/add | solution.py:499
  (5 shorter events, 0.1 us)
Async XLA Ops:
  0.6 3.2 %copy-start.2 = (bf16[192,1000]{1,0:T(8,128)(2,1)S(1)}, bf16[192,1000]{1,0:T(8,128)(2,1)}, u32[]{:S(2)}) copy-start(bf16[192,1000]{1,0:T(8,128)(2,1)} %param.8) | copy-start | bytes 1152004
  0.6 4.2 %copy-start.1 = (bf16[192,1024]{1,0:T(8,128)(2,1)S(1)}, bf16[192,1024]{1,0:T(8,128)(2,1)}, u32[]{:S(2)}) copy-start(bf16[192,1024]{1,0:T(8,128)(2,1)} %param.6) | copy-start | bytes 1179652
  45.1 1.3 copy-start
  118.6 31.9 %copy-start.4 = (s32[192]{0:T(256)S(1)}, s32[192]{0:T(256)}, u32[]{:S(2)}) copy-start(s32[192]{0:T(256)} %param.7) | copy-start | bytes 2308
  150.4 1.9 %copy-start.3 = (s32[2]{0:T(128)S(1)}, s32[2]{0:T(128)}, u32[]{:S(2)}) copy-start(s32[2]{0:T(128)} %param.11) | copy-start | bytes 28

commit v2 on v0

v2 whole, which is shorter than its diff:
```python
import functools

import jax
import jax.numpy as jnp
from jax import lax
from jax.experimental import pallas as pl
from jax.experimental.pallas import tpu as pltpu
from jax.sharding import PartitionSpec as P

MESH = pl.DeviceIdType.MESH
HI = lax.Precision.HIGHEST
F32 = jnp.float32
BF16 = jnp.bfloat16
NX, NY, NZ = 4, 4, 8
BLOCK = 512
CLASSES = 1024
VMEM_LIMIT = 52 * 2**20
COPIES = 138
TILE = 128
TILES = BLOCK // TILE
BELOW = [(i, j) for i in range(TILES) for j in range(i)]
EXACT = dict(precision=HI, preferred_element_type=F32)


class Place:
    def __init__(self):
        rows, rrep = lax.axis_index("rows"), lax.axis_index("rrep")
        self.rows, self.rrep = rows, rrep
        self.y, self.z = rows // NZ, rows % NZ
        self.x, self.c = rrep // 2, rrep % 2

    def at_x(self, d):
        other = (self.x + d) % NX
        return other, (self.rows, other * 2 + self.c)

    def at_y(self, d):
        other = (self.y + d) % NY
        return other, (other * NZ + self.z, self.rrep)

    def at_z(self, d):
        other = (self.z + d) % NZ
        return other, (self.y * NZ + other, self.rrep)

    def partner(self):
        return (self.rows, self.x * 2 + 1 - self.c)

    def greet(self, axes):
        barrier = pltpu.get_barrier_semaphore()
        peers = []
        if "x" in axes:
            peers += [self.at_x(d)[1] for d in range(1, NX)]
        if "y" in axes:
            peers += [self.at_y(d)[1] for d in range(1, NY)]
        if "z" in axes:
            peers += [self.at_z(d)[1] for d in range(1, NZ)]
        if "c" in axes:
            peers += [self.partner()]
        for peer in peers:
            pl.semaphore_signal(barrier, inc=1, device_id=peer, device_id_type=MESH)
        pl.semaphore_wait(barrier, len(peers))


class Sender:
    def __init__(self, send_sems, recv_sems):
        self.send_sems, self.recv_sems = send_sems, recv_sems
        self.copies = []

    def start(self, src, dst, device):
        i = len(self.copies)
        copy = pltpu.make_async_remote_copy(
            src_ref=src,
            dst_ref=dst,
            send_sem=self.send_sems.at[i],
            recv_sem=self.recv_sems.at[i],
            device_id=device,
            device_id_type=MESH,
        )
        copy.start()
        self.copies.append(copy)
        return copy

    def drain(self):
        for copy in self.copies:
            copy.wait_send()


def arrive(copies):
    for copy in copies:
        copy.wait_recv()


def gather_landmarks(me, out, zin, xin, rin, zall, xp, rp, r1, s1, r2):
    x, y, z, c = me.x, me.y, me.z, me.c
    first = []
    for d in range(1, NY):
        other, device = me.at_y(d)
        first.append(out.start(zin.at[other], r1.at[d - 1], device))
    swap = [out.start(xin, xp, me.partner()), out.start(rin, rp, me.partner())]
    arrive(first)
    s1[...] = zin[y] + r1[0] + r1[1] + r1[2]
    second = []
    for d in range(1, NZ):
        other, device = me.at_z(d)
        second.append(out.start(s1.at[other], r2.at[d - 1], device))
    arrive(second)
    total = s1[z]
    for d in range(1, NZ):
        total = total + r2[d - 1]
    s, g = z // 4, z % 4
    zall[y, s, x, c, g] = total
    mine = zall.at[y, s, x, c, g]
    arrive([out.start(mine, mine, me.at_z(d)[1]) for d in range(1, NZ)])
    spread_plane(
        me,
        out,
        lambda i, j: zall.at[j, 0, i, c],
        lambda i, j: zall.at[j, 1, i, c],
        lambda i: zall.at[:, 0, i, c],
        lambda j: zall.at[j, 1, :, c],
    )
    arrive(swap)


def spread_plane(me, out, one_a, one_b, column, row):
    x, y = me.x, me.y
    copies = []
    for d in range(1, 4):
        copies.append(out.start(one_a(x, y), one_a(x, y), me.at_y(d)[1]))
        copies.append(out.start(one_b(x, y), one_b(x, y), me.at_x(d)[1]))
    arrive(copies)
    copies = []
    for d in range(1, 4):
        copies.append(out.start(column(x), column(x), me.at_x(d)[1]))
        copies.append(out.start(row(y), row(y), me.at_y(d)[1]))
    across = [
        out.start(column(x), column(x), me.partner()),
        out.start(row(y), row(y), me.partner()),
    ]
    for d in range(1, 4):
        arrive([copies[2 * d - 2]])
        source = (x - d) % NX
        across.append(out.start(column(source), column(source), me.partner()))
        arrive([copies[2 * d - 1]])
        source = (y - d) % NY
        across.append(out.start(row(source), row(source), me.partner()))
    arrive(across)


CONTRACT = (((0,), (0,)), ((), ()))


def columns_of(zall, xref, kern, start):
    rows = xref.shape[0]
    total = None
    for y in range(NY):
        part = lax.dot_general(
            xref[:, y * 256 : (y + 1) * 256],
            zall[y].reshape(2 * BLOCK, 256),
            (((1,), (1,)), ((), ())),
            preferred_element_type=F32,
        )
        total = part if total is None else total + part
    kern[start : start + rows, :] = jnp.exp(total * (1024**-0.5)).astype(BF16)


def eye_mask():
    rows = lax.broadcasted_iota(jnp.int32, (TILE, TILE), 0)
    cols = lax.broadcasted_iota(jnp.int32, (TILE, TILE), 1)
    return rows, cols


def partial_grams(me, kern, gin, diag):
    base = me.c * BLOCK
    rows, cols = eye_mask()
    diagonal = []
    for i in range(TILES):
        left = kern[:, pl.ds(pl.multiple_of(base + i * TILE, TILE), TILE)]
        right = kern[:, pl.ds(pl.multiple_of(base, TILE), (i + 1) * TILE)]
        panel = lax.dot_general(left, right, CONTRACT, preferred_element_type=F32)
        for j in range(i):
            k = BELOW.index((i, j))
            gin[k // NY, k % NY] = panel[:, j * TILE : (j + 1) * TILE].reshape(NZ, 16, TILE)
        diagonal.append(panel[:, i * TILE : (i + 1) * TILE])
    for k in range(2):
        both = jnp.where(rows >= cols, diagonal[2 * k], diagonal[2 * k + 1])
        gin[1, 2 + k] = both.reshape(NZ, 16, TILE)
        lost = jnp.where(rows == cols, diagonal[2 * k + 1], 0.0)
        diag[k : k + 1, :] = jnp.sum(lost, axis=0, keepdims=True)
    diag[2:, :] = jnp.zeros((6, TILE), F32)
    cross = kern[:, pl.ds(pl.multiple_of(BLOCK + me.c * 256, 256), 256)]
    side = lax.dot_general(cross, kern[:, :BLOCK], CONTRACT, preferred_element_type=F32)
    for i in range(2):
        for j in range(TILES):
            block = side[i * TILE : (i + 1) * TILE, j * TILE : (j + 1) * TILE]
            gin[2 + i, j] = block.reshape(NZ, 16, TILE)


def partial_products(me, kern, rin, rp, pin):
    rows = rin.shape[0]
    mine = pl.ds(pl.multiple_of(me.c * BLOCK, BLOCK), BLOCK)
    for x in range(NX):
        part = slice(x * 256, (x + 1) * 256)
        own = lax.dot_general(rin[:, part], kern[:rows, mine], CONTRACT, preferred_element_type=F32)
        other = lax.dot_general(rp[:, part], kern[rows:, mine], CONTRACT, preferred_element_type=F32)
        pin[x] = (own + other).reshape(NY, 64, BLOCK)


def sum_plane_one(me, out, src, ra, rb, h):
    copies = []
    for d in range(1, 4):
        i, device = me.at_x(d)
        copies.append(out.start(src.at[i, :, 0:h], ra.at[d - 1], device))
        i, device = me.at_y(d)
        copies.append(out.start(src.at[:, i, h : 2 * h], rb.at[d - 1], device))
    return copies


def sum_plane_two(me, out, sa, sb, ra, rb):
    copies = []
    for d in range(1, 4):
        i, device = me.at_y(d)
        copies.append(out.start(sa.at[i], ra.at[d - 1], device))
        i, device = me.at_x(d)
        copies.append(out.start(sb.at[i], rb.at[d - 1], device))
    return copies


def sum_line(me, out, src, received):
    copies = []
    for d in range(1, NZ):
        i, device = me.at_z(d)
        copies.append(out.start(src.at[i], received.at[d - 1], device))
    return copies


def total_of(own, received):
    for d in range(received.shape[0]):
        own = own + received[d]
    return own


def eliminate_rows(values, k, n):
    lane = lax.broadcasted_iota(jnp.int32, (8, n), 1)
    sub = lax.broadcasted_iota(jnp.int32, (8, n), 0)
    rows = values[k : k + 8, :]
    pivots = [jnp.broadcast_to(rows[:, k + q : k + q + 1], (8, n)) for q in range(8)]
    inside = (lane >= k) & (lane < k + 8)
    panel = jnp.where(inside, (lane - k == sub).astype(F32), rows)
    for q in range(8):
        factor = pivots[q]
        inverse = 1.0 / jnp.broadcast_to(factor[q : q + 1, :], (8, n))
        own = sub == q

        def update(block):
            row = jnp.broadcast_to(block[q : q + 1, :], (8, n)) * inverse
            return jnp.where(own, row, block - factor * row)

        for j in range(q + 1, 8):
            pivots[j] = update(pivots[j])
        panel = update(panel)
    return panel


def invert_tile(values, n):
    lane = lax.broadcasted_iota(jnp.int32, (n, n), 1)
    for k in range(0, n, 8):
        panel = eliminate_rows(values, k, n)
        inside = (lane >= k) & (lane < k + 8)
        rest = jnp.where(inside, 0.0, values)
        for q in range(8):
            column = jnp.broadcast_to(values[:, k + q : k + q + 1], (n, n))
            rest = rest - column * jnp.broadcast_to(panel[q : q + 1, :], (n, n))
        parts = ([rest[:k]] if k else []) + [panel] + ([rest[k + 8 :]] if k + 8 < n else [])
        values = jnp.concatenate(parts, axis=0)
    return values


def invert_step(ref, j):
    s = slice(j * TILE, (j + 1) * TILE)
    inverse = invert_tile(ref[s, s], TILE)
    row = jnp.dot(inverse, ref[s, :], **EXACT)
    column = ref[:, s]
    ref[:, s] = jnp.zeros((BLOCK, TILE), F32)
    parts = ([row[:, : j * TILE]] if j else []) + [inverse]
    parts += [row[:, (j + 1) * TILE :]] if j < TILES - 1 else []
    row = jnp.concatenate(parts, axis=1)
    for i in range(TILES):
        t = slice(i * TILE, (i + 1) * TILE)
        if i != j:
            ref[t, :] -= jnp.dot(column[t], row, **EXACT)
    ref[s, :] = row


def unpack_grams(ridge, gall, diag, inv, side):
    rows, cols = eye_mask()
    for k, (i, j) in enumerate(BELOW):
        block = gall[k // NY, k % NY].reshape(TILE, TILE)
        inv[i * TILE : (i + 1) * TILE, j * TILE : (j + 1) * TILE] = block
        inv[j * TILE : (j + 1) * TILE, i * TILE : (i + 1) * TILE] = block.T
    for k in range(2):
        both = gall[1, 2 + k].reshape(TILE, TILE)
        turned = both.T
        lower = jnp.where(rows >= cols, both, turned)
        upper = jnp.where(rows < cols, both, turned)
        upper = jnp.where(rows == cols, diag[k : k + 1, :], upper)
        for i, block in ((2 * k, lower), (2 * k + 1, upper)):
            s = slice(i * TILE, (i + 1) * TILE)
            inv[s, s] = block + jnp.where(rows == cols, ridge, 0.0)
    for i in range(2):
        for j in range(TILES):
            side[i * TILE : (i + 1) * TILE, j * TILE : (j + 1) * TILE] = gall[2 + i, j].reshape(TILE, TILE)


def cross_product(delta, side):
    return lax.dot_general(delta.astype(BF16).astype(F32), side, (((1,), (1,)), ((), ())), **EXACT)


def update_kernel(
    ridge,
    zin, xin, rin,
    kout, dout,
    zall, xp, rp, r1, s1, r2,
    kern, gin, diag, pin,
    ga1, gb1, ga, gb, ga2, gb2, g2, g3, gall,
    dx, dxs, dy, dys, dz,
    pa1, pb1, pa, pb, pa2, pb2, p2, p3, prod,
    inv, side, delta, part, other, opart,
    send_sems, recv_sems,
):
    me = Place()
    me.greet("xyzc")
    out = Sender(send_sems, recv_sems)
    x, y, z, c = me.x, me.y, me.z, me.c
    rows = xin.shape[0]
    gather_landmarks(me, out, zin, xin, rin, zall, xp, rp, r1, s1, r2)
    columns_of(zall, xin, kern, 0)
    columns_of(zall, xp, kern, rows)
    partial_grams(me, kern, gin, diag)

    grams = sum_plane_one(me, out, gin, ga1, gb1, 4)
    diags = [out.start(diag, dx.at[d - 1], me.at_x(d)[1]) for d in range(1, NX)]
    kout[...] = kern[:rows, :]
    partial_products(me, kern, rin, rp, pin)
    arrive(grams)
    ga[...] = total_of(gin[x, :, 0:4], ga1)
    gb[...] = total_of(gin[:, y, 4:8], gb1)
    grams = sum_plane_two(me, out, ga, gb, ga2, gb2)
    arrive(diags)
    dxs[...] = total_of(diag[...], dx)
    diags = [out.start(dxs, dy.at[d - 1], me.at_y(d)[1]) for d in range(1, NY)]
    arrive(grams)
    g2[0:4] = total_of(ga[y], ga2)
    g2[4:8] = total_of(gb[x], gb2)
    grams = sum_line(me, out, g2, g3)
    products = sum_plane_one(me, out, pin, pa1, pb1, 32)
    arrive(diags)
    dys[...] = total_of(dxs[...], dy)
    diags = [out.start(dys, dz.at[d - 1], me.at_z(d)[1]) for d in range(1, NZ)]
    arrive(grams)
    gall[x, y, z] = total_of(g2[z], g3)
    mine = gall.at[x, y, z]
    grams = [out.start(mine, mine, me.at_z(d)[1]) for d in range(1, NZ)]
    arrive(grams)
    grams = []
    for d in range(1, 4):
        grams.append(out.start(gall.at[x, y, 0:4], gall.at[x, y, 0:4], me.at_y(d)[1]))
        grams.append(out.start(gall.at[x, y, 4:8], gall.at[x, y, 4:8], me.at_x(d)[1]))
    arrive(products)
    pa[...] = total_of(pin[x, :, 0:32], pa1)
    pb[...] = total_of(pin[:, y, 32:64], pb1)
    arrive(grams)
    grams = []
    for d in range(1, 4):
        grams.append(out.start(gall.at[x, :, 0:4], gall.at[x, :, 0:4], me.at_x(d)[1]))
        grams.append(out.start(gall.at[:, y, 4:8], gall.at[:, y, 4:8], me.at_y(d)[1]))
    products = sum_plane_two(me, out, pa, pb, pa2, pb2)
    arrive(diags)
    lost = total_of(dys[...], dz)
    arrive(grams)

    unpack_grams(ridge, gall, lost, inv, side)
    invert_step(inv, 0)
    arrive(products)
    p2[0:4] = total_of(pa[y], pa2).reshape(4, 8, BLOCK)
    p2[4:8] = total_of(pb[x], pb2).reshape(4, 8, BLOCK)
    products = sum_line(me, out, p2, p3)
    invert_step(inv, 1)
    invert_step(inv, 2)
    arrive(products)
    prod[z] = total_of(p2[z], p3)
    products = [out.start(prod.at[z], prod.at[z], me.at_z(d)[1]) for d in range(1, NZ)]
    invert_step(inv, 3)
    arrive(products)

    target = prod[...].reshape(64, BLOCK)
    first = jnp.dot(target, inv[...], **EXACT)
    delta[...] = first
    swap = [out.start(delta, other, me.partner())]
    part[...] = cross_product(first, side[...])
    swap.append(out.start(part, opart, me.partner()))
    arrive(swap[:1])
    here = cross_product(other[...], side[...])
    arrive(swap[1:])
    cross = jnp.concatenate([opart[...], here], axis=1)
    second = jnp.dot(target - cross, inv[...], **EXACT)
    dout[c, x, y] = jnp.where(c == 0, first, second).astype(BF16)
    spread_plane(
        me,
        out,
        lambda i, j: dout.at[c, i, j, 0:32],
        lambda i, j: dout.at[c, i, j, 32:64],
        lambda i: dout.at[c, i, :, 0:32],
        lambda j: dout.at[c, :, j, 32:64],
    )
    out.drain()


def update(zin, xhat, rounded, ridge):
    rows = xhat.shape[0]
    vmem = pl.BlockSpec(memory_space=pltpu.VMEM)
    wide = lambda *shape: pltpu.VMEM(shape, F32)
    half = lambda *shape: pltpu.VMEM(shape, BF16)
    return pl.pallas_call(
        functools.partial(update_kernel, ridge),
        out_shape=(
            jax.ShapeDtypeStruct((rows, 2 * BLOCK), BF16),
            jax.ShapeDtypeStruct((2, NX, NY, 64, BLOCK), BF16),
        ),
        in_specs=[vmem] * 3,
        out_specs=(vmem,) * 2,
        scratch_shapes=[
            half(NY, 2, NX, 2, 4, 16, 256),
            half(rows, 1024),
            half(rows, CLASSES),
            half(NY - 1, NZ, 16, 256),
            half(NZ, 16, 256),
            half(NZ - 1, 16, 256),
            half(2 * rows, 2 * BLOCK),
            wide(NX, NY, NZ, 16, TILE),
            wide(8, TILE),
            wide(NX, NY, 64, BLOCK),
            wide(3, 4, 4, 16, TILE),
            wide(3, 4, 4, 16, TILE),
            wide(4, 4, 16, TILE),
            wide(4, 4, 16, TILE),
            wide(3, 4, 16, TILE),
            wide(3, 4, 16, TILE),
            wide(NZ, 16, TILE),
            wide(NZ - 1, 16, TILE),
            wide(NX, NY, NZ, 16, TILE),
            wide(3, 8, TILE),
            wide(8, TILE),
            wide(3, 8, TILE),
            wide(8, TILE),
            wide(NZ - 1, 8, TILE),
            wide(3, 4, 32, BLOCK),
            wide(3, 4, 32, BLOCK),
            wide(4, 32, BLOCK),
            wide(4, 32, BLOCK),
            wide(3, 32, BLOCK),
            wide(3, 32, BLOCK),
            wide(NZ, 8, BLOCK),
            wide(NZ - 1, 8, BLOCK),
            wide(NZ, 8, BLOCK),
            wide(BLOCK, BLOCK),
            wide(256, BLOCK),
            wide(64, BLOCK),
            wide(64, 256),
            wide(64, BLOCK),
            wide(64, 256),
            pltpu.SemaphoreType.DMA((COPIES,)),
            pltpu.SemaphoreType.DMA((COPIES,)),
        ],
        compiler_params=pltpu.CompilerParams(
            collective_id=0, has_side_effects=True, vmem_limit_bytes=VMEM_LIMIT
        ),
        name="update",
    )(zin, xhat, rounded)


def unit_normalize(values):
    wide = values.astype(F32)
    scale = lax.rsqrt(jnp.mean(wide * wide, axis=1, keepdims=True) + 1e-06)
    return (wide * scale).astype(BF16)


def shards(features, labels, scores, landmarks, coefficients, block_ids):
    count = coefficients.shape[1]
    devices_all = lax.axis_size("rows") * lax.axis_size("rrep")
    ridge = float(features.shape[0] * devices_all)
    holder = lax.axis_index("rows")
    replica = lax.axis_index("rrep")
    xhat = unit_normalize(features)
    classes = jnp.arange(count, dtype=jnp.int32)
    residual = (labels[:, None] == classes[None, :]).astype(F32) - scores.astype(F32)
    rounded = jnp.pad(residual.astype(BF16), ((0, 0), (0, CLASSES - count)))
    share = landmarks.shape[0] // 8
    zslice = unit_normalize(lax.dynamic_slice_in_dim(landmarks, replica * share, share, 0))
    mine = (block_ids == holder)[:, None, None]
    zin = jnp.where(mine, zslice[None], jnp.zeros_like(zslice)[None])
    zin = zin.reshape(2, 4, 16, NY, 256).transpose(3, 0, 1, 2, 4).reshape(NY, NZ, 16, 256)
    kern, deltas = update(zin, xhat, rounded, ridge)
    deltas = deltas.reshape(2, CLASSES, BLOCK)[:, :count]
    new_coefficients = coefficients
    for step in range(2):
        added = jnp.where(holder == block_ids[step], deltas[step].T.astype(F32), 0.0)
        new_coefficients = new_coefficients + added
        residual = residual - lax.dot_general(
            kern[:, step * BLOCK : (step + 1) * BLOCK],
            deltas[step],
            (((1,), (1,)), ((), ())),
            preferred_element_type=F32,
        )
    return (new_coefficients, residual)


def solution(mesh):
    in_specs = (
        P(("rows", "rrep"), None),
        P(("rows", "rrep")),
        P(("rows", "rrep"), None),
        P("rows", None),
        P("rows", None),
        P(),
    )
    out_specs = (P("rows", None), P(("rows", "rrep"), None))
    return jax.shard_map(shards, mesh=mesh, in_specs=in_specs, out_specs=out_specs, check_vma=False)
```

time: 1060 us -> 142 us (0.13)
  waiting for transfers between devices: 680 us -> 0 us
  other arithmetic: 263 us -> 6.13 us
  Pallas kernels: 0 us -> 129 us
  matrix products: 55.9 us -> 3.24 us
  local copies, waits for them, and re-layouts: 30.6 us -> 1.66 us
  between operations: 21.4 us -> 2.08 us
    psum x3 -> x0, waiting for transfers between devices: 680 us -> none  [the longest x2 526 us: shards(): summed = lax.psum(stacked, ('rows', 'rrep'))]
    another operation x34 -> x0, other arithmetic: 246 us -> none  [the longest x29 165 us: ridge_solve(): cholesky_factor = jnp.linalg.cholesky(gram + ridge)]
    pallas_call x0 -> x1, Pallas kernels: none -> 129 us  [update(): pl.pallas_call(functools.partial(update_kernel, ridge), out_shape=(jax.Sh...]
    another operation x40 -> x0, matrix products: 49 us -> none  [the longest x28 40 us: ridge_solve(): return jax.scipy.linalg.cho_solve((cholesky_factor, True), product)]
    another operation x35 -> x0, local copies, waits for them, and re-layouts: 24.1 us -> none  [the longest x27 23.2 us: ridge_solve(): return jax.scipy.linalg.cho_solve((cholesky_factor, True), product)]
  transfers between devices with their start and end apart: 3 -> 0, of which waited for: 3 -> 0; matrix products, arithmetic and copies ran while one was open for 0% -> 0% of each run, Pallas kernels for 0% -> 0%
where the time goes in v2:
time: 142 us
  Pallas kernels  129 us (91%)
  other arithmetic  6.13 us (4%)
  matrix products  3.24 us (2%)
  between operations  2.08 us (1%)
  local copies, waits for them, and re-layouts  1.66 us (1%)
    pallas_call x1, Pallas kernels, update(): pl.pallas_call(functools.partial(update_kernel, ridge), out_shape=(jax.Sh...  129 us
    dot_general x2, matrix products, shards(): lax.dot_general(kern[:, step * BLOCK:(step + 1) * BLOCK], deltas[step], (...  3.24 us

profile of v2, /device:TPU:1, one launch (start us, length us, event | category | flops | bytes accessed | tf_op | source)
XLA Modules:
  0.0 141.8 jit_solution(8615653789752303842)
XLA Ops:
  0.6 0.0 copy-start.3
  0.6 0.0 copy-start.4
  0.6 0.0 copy-start.2
  0.7 1.1 fusion.3
  1.8 0.7 broadcast_compare_fusion
  2.5 0.1 broadcast_in_dim.45
  2.5 0.1 broadcast_in_dim.46
  2.6 1.2 fusion
  3.8 1.3 fusion.7
  6.4 1.0 fusion.4
  7.4 0.1 broadcast_in_dim.48
  7.5 0.1 broadcast_select_fusion.zin
  7.6 0.0 copy-done.2
  7.6 0.1 fusion.1.xin
  7.8 0.0 copy-done.3
  7.8 0.0 copy-done.4
  7.8 0.2 fusion.2
  8.1 128.7 %update.1 = (bf16[192,1024]{1,0:T(8,128)(2,1)S(1)}, bf16[2,4,4,64,512]{4,3,2,1,0:T(8,128)(2,1)}) custom-call(bf16[4,8,16,256]{3,2,1,0:T(8,128)(2,1)S(1)} %broadcast_select_fusion.zin, bf16[192,1024]{1,0:T(8,128)(2,1)S(1)} %fusion.1.xin, bf16[192,1024]{1,0:T(8,128)(2,1)S(1)} %pad.4.rin), custom_call_target="tpu_custom_call" | custom-call | tf_op jit(solution)/shard_map/update/pallas_call | solution.py:423
  136.8 0.0 copy-start
  136.8 0.0 copy-start.1
  136.8 1.9 %convolution_subtract_fusion.1 = f32[192,1000]{1,0:T(8,128)S(1)} fusion(bf16[2,1024,512]{2,1,0:T(8,128)(2,1)} %bitcast.21, bf16[192,1000]{1,0:T(8,128)(2,1)S(1)} %copy-done.3, s32[192]{0:T(256)S(1)} %copy-done.4, bf16[192,1024]{1,0:T(8,128)(2,1)S(1)} %get-tuple-element.5), kind=kOutput, calls=%fused_computation.3 | convolution fusion | flops 197568000 | bytes 2382848 | tf_op jit(solution)/shard_map/dot_general | solution.py:508
  138.7 0.0 copy-done
  138.7 1.4 convolution_subtract_fusion
  140.1 0.0 copy-done.1
  140.1 1.8 %bitcast_add_fusion = f32[512,1000]{0,1:T(8,128)} fusion(f32[512,1000]{0,1:T(8,128)S(1)} %copy-done.1, pred[]{:T(512)S(6)} %eq.31, pred[]{:T(512)S(6)} %eq.25, bf16[2,1024,512]{2,1,0:T(8,128)(2,1)S(1)} %bitcast.23), kind=kLoop, calls=%fused_computation | loop fusion | flops 3072000 | bytes 6144002 | tf_op jit(solution)/shard_map/add | solution.py:507
  (5 shorter events, 0.1 us)
Async XLA Ops:
  0.6 7.2 %copy-start.3 = (bf16[192,1000]{1,0:T(8,128)(2,1)S(1)}, bf16[192,1000]{1,0:T(8,128)(2,1)}, u32[]{:S(2)}) copy-start(bf16[192,1000]{1,0:T(8,128)(2,1)} %param.8) | copy-start | bytes 1152004
  0.6 7.2 %copy-start.4 = (s32[192]{0:T(256)S(1)}, s32[192]{0:T(256)}, u32[]{:S(2)}) copy-start(s32[192]{0:T(256)} %param.7) | copy-start | bytes 2308
  0.6 7.0 %copy-start.2 = (bf16[192,1024]{1,0:T(8,128)(2,1)S(1)}, bf16[192,1024]{1,0:T(8,128)(2,1)}, u32[]{:S(2)}) copy-start(bf16[192,1024]{1,0:T(8,128)(2,1)} %param.6) | copy-start | bytes 1179652
  136.8 1.9 %copy-start = (bf16[2,4,4,64,512]{4,3,2,1,0:T(8,128)(2,1)S(1)}, bf16[2,4,4,64,512]{4,3,2,1,0:T(8,128)(2,1)}, u32[]{:S(2)}) copy-start(bf16[2,4,4,64,512]{4,3,2,1,0:T(8,128)(2,1)} %get-tuple-element.4) | copy-start | bytes 6291460
  136.8 3.3 %copy-start.1 = (f32[512,1000]{0,1:T(8,128)S(1)}, f32[512,1000]{0,1:T(8,128)}, u32[]{:S(2)}) copy-start(f32[512,1000]{0,1:T(8,128)} %param.10) | copy-start | bytes 6144004

commit v3 on v2

--- a/solution.py
+++ b/solution.py
@@ -65,7 +65,7 @@
         self.send_sems, self.recv_sems = send_sems, recv_sems
         self.copies = []
 
-    def start(self, src, dst, device):
+    def make(self, src, dst, device):
         i = len(self.copies)
         copy = pltpu.make_async_remote_copy(
             src_ref=src,
@@ -75,8 +75,12 @@
             device_id=device,
             device_id_type=MESH,
         )
+        self.copies.append(copy)
+        return copy
+
+    def start(self, src, dst, device):
+        copy = self.make(src, dst, device)
         copy.start()
-        self.copies.append(copy)
         return copy
 
     def drain(self):
@@ -89,12 +93,40 @@
         copy.wait_recv()
 
 
-def gather_landmarks(me, out, zin, xin, rin, zall, xp, rp, r1, s1, r2):
+def unit_normalize(values):
+    wide = values.astype(F32)
+    scale = lax.rsqrt(jnp.mean(wide * wide, axis=1, keepdims=True) + 1e-06)
+    return (wide * scale).astype(BF16)
+
+
+def masked_landmarks(me, block_ids, lands, zin):
+    share = unit_normalize(lands[...])
+    for s in range(2):
+        held = jnp.where(block_ids[s] == me.rows, 1.0, 0.0).astype(BF16)
+        kept = share * held
+        for y in range(NY):
+            for g in range(4):
+                zin[y, s * 4 + g] = kept[g * 16 : (g + 1) * 16, y * 256 : (y + 1) * 256]
+
+
+def own_rows(features, labels, scores, xin, rin):
+    count = scores.shape[1]
+    xin[...] = unit_normalize(features[...])
+    classes = lax.broadcasted_iota(jnp.int32, scores.shape, 1)
+    target = jnp.where(classes == labels[...], 1.0, 0.0)
+    rin[:, CLASSES - 128 :] = jnp.zeros((rin.shape[0], 128), BF16)
+    rin[:, :count] = (target - scores[...].astype(F32)).astype(BF16)
+
+
+def gather_landmarks(me, out, zin, rows, fetches, xin, rin, zall, xp, rp, r1, s1, r2):
     x, y, z, c = me.x, me.y, me.z, me.c
     first = []
     for d in range(1, NY):
         other, device = me.at_y(d)
         first.append(out.start(zin.at[other], r1.at[d - 1], device))
+    for fetch in fetches:
+        fetch.wait()
+    own_rows(*rows, xin, rin)
     swap = [out.start(xin, xp, me.partner()), out.start(rin, rp, me.partner())]
     arrive(first)
     s1[...] = zin[y] + r1[0] + r1[1] + r1[2]
@@ -198,11 +230,15 @@
 def partial_products(me, kern, rin, rp, pin):
     rows = rin.shape[0]
     mine = pl.ds(pl.multiple_of(me.c * BLOCK, BLOCK), BLOCK)
-    for x in range(NX):
-        part = slice(x * 256, (x + 1) * 256)
+
+    def step(x, carry):
+        part = pl.ds(pl.multiple_of(x * 256, 256), 256)
         own = lax.dot_general(rin[:, part], kern[:rows, mine], CONTRACT, preferred_element_type=F32)
         other = lax.dot_general(rp[:, part], kern[rows:, mine], CONTRACT, preferred_element_type=F32)
         pin[x] = (own + other).reshape(NY, 64, BLOCK)
+        return carry
+
+    lax.fori_loop(0, NX, step, 0)
 
 
 def sum_plane_one(me, out, src, ra, rb, h):
@@ -275,20 +311,22 @@
     return values
 
 
-def invert_step(ref, j):
-    s = slice(j * TILE, (j + 1) * TILE)
-    inverse = invert_tile(ref[s, s], TILE)
-    row = jnp.dot(inverse, ref[s, :], **EXACT)
-    column = ref[:, s]
-    ref[:, s] = jnp.zeros((BLOCK, TILE), F32)
-    parts = ([row[:, : j * TILE]] if j else []) + [inverse]
-    parts += [row[:, (j + 1) * TILE :]] if j < TILES - 1 else []
-    row = jnp.concatenate(parts, axis=1)
-    for i in range(TILES):
-        t = slice(i * TILE, (i + 1) * TILE)
-        if i != j:
-            ref[t, :] -= jnp.dot(column[t], row, **EXACT)
-    ref[s, :] = row
+def invert(ref, row, halfway):
+    def step(j, carry):
+        pl.when(j == TILES // 2)(halfway)
+        s = pl.ds(pl.multiple_of(j * TILE, TILE), TILE)
+        inverse = invert_tile(ref[s, s], TILE)
+        row[...] = jnp.dot(inverse, ref[s, :], **EXACT)
+        row[:, s] = inverse
+        column = ref[:, s]
+        ref[:, s] = jnp.zeros((BLOCK, TILE), F32)
+        for i in range(TILES):
+            t = slice(i * TILE, (i + 1) * TILE)
+            ref[t, :] -= jnp.dot(column[t], row[...], **EXACT)
+        ref[s, :] = row[...]
+        return carry
+
+    lax.fori_loop(0, TILES, step, 0)
 
 
 def unpack_grams(ridge, gall, diag, inv, side):
@@ -317,22 +355,39 @@
 
 def update_kernel(
     ridge,
-    zin, xin, rin,
+    block_ids, lands_all, features_all, labels_all, scores_all,
     kout, dout,
-    zall, xp, rp, r1, s1, r2,
+    lands, features, labels, scores, fetch_sems, zin, xin, rin, zall, xp, rp, r1, s1, r2,
     kern, gin, diag, pin,
     ga1, gb1, ga, gb, ga2, gb2, g2, g3, gall,
     dx, dxs, dy, dys, dz,
     pa1, pb1, pa, pb, pa2, pb2, p2, p3, prod,
-    inv, side, delta, part, other, opart,
+    inv, pivots, side, delta, part, other, opart,
     send_sems, recv_sems,
 ):
     me = Place()
+    share = lands.shape[0]
+    start = pl.multiple_of(me.rrep * share, share)
+    fetches = [
+        pltpu.make_async_copy(src, dst, fetch_sems.at[i])
+        for i, (src, dst) in enumerate(
+            (
+                (lands_all.at[pl.ds(start, share)], lands),
+                (features_all, features),
+                (labels_all, labels),
+                (scores_all, scores),
+            )
+        )
+    ]
+    for fetch in fetches:
+        fetch.start()
+    fetches[0].wait()
+    masked_landmarks(me, block_ids, lands, zin)
     me.greet("xyzc")
     out = Sender(send_sems, recv_sems)
     x, y, z, c = me.x, me.y, me.z, me.c
     rows = xin.shape[0]
-    gather_landmarks(me, out, zin, xin, rin, zall, xp, rp, r1, s1, r2)
+    gather_landmarks(me, out, zin, (features, labels, scores), fetches[1:], xin, rin, zall, xp, rp, r1, s1, r2)
     columns_of(zall, xin, kern, 0)
     columns_of(zall, xp, kern, rows)
     partial_grams(me, kern, gin, diag)
@@ -379,18 +434,20 @@
     arrive(grams)
 
     unpack_grams(ridge, gall, lost, inv, side)
-    invert_step(inv, 0)
     arrive(products)
     p2[0:4] = total_of(pa[y], pa2).reshape(4, 8, BLOCK)
     p2[4:8] = total_of(pb[x], pb2).reshape(4, 8, BLOCK)
     products = sum_line(me, out, p2, p3)
-    invert_step(inv, 1)
-    invert_step(inv, 2)
-    arrive(products)
-    prod[z] = total_of(p2[z], p3)
-    products = [out.start(prod.at[z], prod.at[z], me.at_z(d)[1]) for d in range(1, NZ)]
-    invert_step(inv, 3)
-    arrive(products)
+    returns = [out.make(prod.at[z], prod.at[z], me.at_z(d)[1]) for d in range(1, NZ)]
+
+    def halfway():
+        arrive(products)
+        prod[z] = total_of(p2[z], p3)
+        for copy in returns:
+            copy.start()
+
+    invert(inv, pivots, halfway)
+    arrive(returns)
 
     target = prod[...].reshape(64, BLOCK)
     first = jnp.dot(target, inv[...], **EXACT)
@@ -415,8 +472,9 @@
     out.drain()
 
 
-def update(zin, xhat, rounded, ridge):
-    rows = xhat.shape[0]
+def update(block_ids, landmarks, features, labels, scores, ridge):
+    rows = features.shape[0]
+    share = landmarks.shape[0] // 8
     vmem = pl.BlockSpec(memory_space=pltpu.VMEM)
     wide = lambda *shape: pltpu.VMEM(shape, F32)
     half = lambda *shape: pltpu.VMEM(shape, BF16)
@@ -426,9 +484,17 @@
             jax.ShapeDtypeStruct((rows, 2 * BLOCK), BF16),
             jax.ShapeDtypeStruct((2, NX, NY, 64, BLOCK), BF16),
         ),
-        in_specs=[vmem] * 3,
+        in_specs=[pl.BlockSpec(memory_space=pltpu.SMEM)] + [pl.BlockSpec(memory_space=pl.ANY)] * 4,
         out_specs=(vmem,) * 2,
         scratch_shapes=[
+            half(share, 1024),
+            half(rows, 1024),
+            pltpu.VMEM((rows, 1), jnp.int32),
+            half(rows, scores.shape[1]),
+            pltpu.SemaphoreType.DMA((4,)),
+            half(NY, NZ, 16, 256),
+            half(rows, 1024),
+            half(rows, CLASSES),
             half(NY, 2, NX, 2, 4, 16, 256),
             half(rows, 1024),
             half(rows, CLASSES),
@@ -463,6 +529,7 @@
             wide(NZ - 1, 8, BLOCK),
             wide(NZ, 8, BLOCK),
             wide(BLOCK, BLOCK),
+            wide(TILE, BLOCK),
             wide(256, BLOCK),
             wide(64, BLOCK),
             wide(64, 256),
@@ -475,13 +542,7 @@
             collective_id=0, has_side_effects=True, vmem_limit_bytes=VMEM_LIMIT
         ),
         name="update",
-    )(zin, xhat, rounded)
-
-
-def unit_normalize(values):
-    wide = values.astype(F32)
-    scale = lax.rsqrt(jnp.mean(wide * wide, axis=1, keepdims=True) + 1e-06)
-    return (wide * scale).astype(BF16)
+    )(block_ids, landmarks, features, labels, scores)
 
 
 def shards(features, labels, scores, landmarks, coefficients, block_ids):
@@ -489,17 +550,9 @@
     devices_all = lax.axis_size("rows") * lax.axis_size("rrep")
     ridge = float(features.shape[0] * devices_all)
     holder = lax.axis_index("rows")
-    replica = lax.axis_index("rrep")
-    xhat = unit_normalize(features)
     classes = jnp.arange(count, dtype=jnp.int32)
     residual = (labels[:, None] == classes[None, :]).astype(F32) - scores.astype(F32)
-    rounded = jnp.pad(residual.astype(BF16), ((0, 0), (0, CLASSES - count)))
-    share = landmarks.shape[0] // 8
-    zslice = unit_normalize(lax.dynamic_slice_in_dim(landmarks, replica * share, share, 0))
-    mine = (block_ids == holder)[:, None, None]
-    zin = jnp.where(mine, zslice[None], jnp.zeros_like(zslice)[None])
-    zin = zin.reshape(2, 4, 16, NY, 256).transpose(3, 0, 1, 2, 4).reshape(NY, NZ, 16, 256)
-    kern, deltas = update(zin, xhat, rounded, ridge)
+    kern, deltas = update(block_ids, landmarks, features, labels[:, None], scores, ridge)
     deltas = deltas.reshape(2, CLASSES, BLOCK)[:, :count]
     new_coefficients = coefficients
     for step in range(2):

time: 142 us -> 134 us (0.944)
  Pallas kernels: 129 us -> 122 us
  other arithmetic: 6.13 us -> 1.75 us
  local copies, waits for them, and re-layouts: 1.66 us -> 4.77 us
    pallas_call x1, Pallas kernels: 129 us -> 122 us  [update(): pl.pallas_call(functools.partial(update_kernel, ridge), out_shape=(jax.Sh...]
    unnamed x10 -> x12, local copies, waits for them, and re-layouts: 0.03 us -> 2.66 us
    reduce_sum x2 -> x0, other arithmetic: 2.26 us -> none  [unit_normalize(): scale = lax.rsqrt(jnp.mean(wide * wide, axis=1, keepdims=True) + 1e-06)]
where the time goes in v3:
time: 134 us
  Pallas kernels  122 us (91%)
  local copies, waits for them, and re-layouts  4.77 us (4%)
  matrix products  3.24 us (2%)
  between operations  2.01 us (1%)
  other arithmetic  1.75 us (1%)
    pallas_call x1, Pallas kernels, update(): pl.pallas_call(functools.partial(update_kernel, ridge), out_shape=(jax.Sh...  122 us
    dot_general x2, matrix products, shards(): lax.dot_general(kern[:, step * BLOCK:(step + 1) * BLOCK], deltas[step], (...  3.24 us

profile of v3, /device:TPU:1, one launch (start us, length us, event | category | flops | bytes accessed | tf_op | source)
XLA Modules:
  0.0 134.2 jit_solution(17426597391396927664)
XLA Ops:
  0.6 0.0 copy-start.5
  0.6 1.3 fusion.2
  3.3 0.8 copy.8.labels_all
  4.1 0.0 copy-start
  4.1 1.0 copy-done
  5.1 0.0 copy-start.1
  5.1 1.0 copy-done.1
  6.1 0.0 copy-start.2
  6.1 0.7 copy-done.2
  6.7 122.4 %update.1 = (bf16[192,1024]{1,0:T(8,128)(2,1)S(1)}, bf16[2,4,4,64,512]{4,3,2,1,0:T(8,128)(2,1)}) custom-call(s32[2]{0:T(128)S(1)} %copy-done.2, bf16[512,1024]{1,0:T(8,128)(2,1)} %lands_all.1, bf16[192,1024]{1,0:T(8,128)(2,1)S(1)} %copy-done, s32[192,1]{1,0:T(8,128)S(1)} %copy.8.labels_all, bf16[192,1000]{1,0:T(8,128)(2,1)S(1)} %copy-done.1), custom_call_target="tpu_custom_call" | custom-call | tf_op jit(solution)/shard_map/update/pallas_call | solution.py:481
  129.2 0.0 copy-start.3
  129.2 0.0 copy-done.5
  129.2 0.0 copy-start.4
  129.2 1.9 %convolution_subtract_fusion.1 = f32[192,1000]{1,0:T(8,128)S(1)} fusion(bf16[2,1024,512]{2,1,0:T(8,128)(2,1)} %bitcast.20, bf16[192,1000]{1,0:T(8,128)(2,1)S(1)} %copy-done.1, s32[192]{0:T(256)S(1)} %copy-done.5, bf16[192,1024]{1,0:T(8,128)(2,1)S(1)} %get-tuple-element.5), kind=kOutput, calls=%fused_computation.3 | convolution fusion | flops 197568000 | bytes 2382848 | tf_op jit(solution)/shard_map/dot_general | solution.py:561
  131.1 0.0 copy-done.3
  131.1 1.4 %convolution_subtract_fusion = f32[192,1000]{1,0:T(8,128)} fusion(f32[192,1000]{1,0:T(8,128)S(1)} %convolution_subtract_fusion.1, bf16[2,1024,512]{2,1,0:T(8,128)(2,1)S(1)} %bitcast.21, bf16[192,1024]{1,0:T(8,128)(2,1)S(1)} %get-tuple-element.5), kind=kOutput, calls=%fused_computation.2 | convolution fusion | flops 196800000 | bytes 2775040 | tf_op jit(solution)/shard_map/dot_general | solution.py:561
  132.4 0.0 copy-done.4
  132.4 1.8 %bitcast_add_fusion = f32[512,1000]{0,1:T(8,128)} fusion(f32[512,1000]{0,1:T(8,128)S(1)} %copy-done.4, pred[]{:T(512)S(6)} %eq.20, pred[]{:T(512)S(6)} %eq.19, bf16[2,1024,512]{2,1,0:T(8,128)(2,1)S(1)} %bitcast.22), kind=kLoop, calls=%fused_computation | loop fusion | flops 3072000 | bytes 6144002 | tf_op jit(solution)/shard_map/add | solution.py:560
Async XLA Ops:
  0.6 128.5 %copy-start.5 = (s32[192]{0:T(256)S(1)}, s32[192]{0:T(256)}, u32[]{:S(2)}) copy-start(s32[192]{0:T(256)} %param.7) | copy-start | bytes 2308
  4.1 1.0 copy-start
  5.1 1.0 copy-start.1
  6.1 0.7 copy-start.2
  129.2 1.9 %copy-start.3 = (bf16[2,4,4,64,512]{4,3,2,1,0:T(8,128)(2,1)S(1)}, bf16[2,4,4,64,512]{4,3,2,1,0:T(8,128)(2,1)}, u32[]{:S(2)}) copy-start(bf16[2,4,4,64,512]{4,3,2,1,0:T(8,128)(2,1)} %get-tuple-element.4) | copy-start | bytes 6291460
  129.2 3.3 %copy-start.4 = (f32[512,1000]{0,1:T(8,128)S(1)}, f32[512,1000]{0,1:T(8,128)}, u32[]{:S(2)}) copy-start(f32[512,1000]{0,1:T(8,128)} %param.10) | copy-start | bytes 6144004

commit v4 on v3

--- a/solution.py
+++ b/solution.py
@@ -57,7 +57,7 @@
             peers += [self.partner()]
         for peer in peers:
             pl.semaphore_signal(barrier, inc=1, device_id=peer, device_id_type=MESH)
-        pl.semaphore_wait(barrier, len(peers))
+        return barrier, len(peers)
 
 
 class Sender:
@@ -109,11 +109,20 @@
                 zin[y, s * 4 + g] = kept[g * 16 : (g + 1) * 16, y * 256 : (y + 1) * 256]
 
 
+def onehot(labels, shape):
+    n = shape[0]
+    rows = lax.broadcasted_iota(jnp.int32, (n, n), 0)
+    cols = lax.broadcasted_iota(jnp.int32, (n, n), 1)
+    spread = jnp.where(rows == cols, jnp.broadcast_to(labels, (n, n)).astype(F32), 0.0)
+    column = jnp.sum(spread, axis=1, keepdims=True)
+    classes = lax.broadcasted_iota(jnp.int32, shape, 1).astype(F32)
+    return jnp.where(classes == column, 1.0, 0.0)
+
+
 def own_rows(features, labels, scores, xin, rin):
     count = scores.shape[1]
     xin[...] = unit_normalize(features[...])
-    classes = lax.broadcasted_iota(jnp.int32, scores.shape, 1)
-    target = jnp.where(classes == labels[...], 1.0, 0.0)
+    target = onehot(labels[...], scores.shape)
     rin[:, CLASSES - 128 :] = jnp.zeros((rin.shape[0], 128), BF16)
     rin[:, :count] = (target - scores[...].astype(F32)).astype(BF16)
 
@@ -366,6 +375,7 @@
     send_sems, recv_sems,
 ):
     me = Place()
+    greeted = me.greet("xyzc")
     share = lands.shape[0]
     start = pl.multiple_of(me.rrep * share, share)
     fetches = [
@@ -383,7 +393,7 @@
         fetch.start()
     fetches[0].wait()
     masked_landmarks(me, block_ids, lands, zin)
-    me.greet("xyzc")
+    pl.semaphore_wait(*greeted)
     out = Sender(send_sems, recv_sems)
     x, y, z, c = me.x, me.y, me.z, me.c
     rows = xin.shape[0]
@@ -484,12 +494,12 @@
             jax.ShapeDtypeStruct((rows, 2 * BLOCK), BF16),
             jax.ShapeDtypeStruct((2, NX, NY, 64, BLOCK), BF16),
         ),
-        in_specs=[pl.BlockSpec(memory_space=pltpu.SMEM)] + [pl.BlockSpec(memory_space=pl.ANY)] * 4,
+        in_specs=[pl.BlockSpec(memory_space=pltpu.SMEM)] + [pl.BlockSpec(memory_space=pltpu.HBM)] * 4,
         out_specs=(vmem,) * 2,
         scratch_shapes=[
             half(share, 1024),
             half(rows, 1024),
-            pltpu.VMEM((rows, 1), jnp.int32),
+            pltpu.VMEM((1, rows), jnp.int32),
             half(rows, scores.shape[1]),
             pltpu.SemaphoreType.DMA((4,)),
             half(NY, NZ, 16, 256),
@@ -545,26 +555,69 @@
     )(block_ids, landmarks, features, labels, scores)
 
 
+def finish_kernel(block_ids, kern, deltas, labels, scores, old, new, residual, old_tiles, new_tiles, rest, fetch_sems, store_sems):
+    count = scores.shape[1]
+    holder = lax.axis_index("rows")
+    size = count // 5
+    parts = [slice(i * size, (i + 1) * size) for i in range(5)]
+    fetches = [
+        pltpu.make_async_copy(old.at[parts[i]], old_tiles.at[i], fetch_sems.at[i]) for i in range(5)
+    ]
+    for fetch in fetches:
+        fetch.start()
+    total = onehot(labels[...], scores.shape) - scores[...].astype(F32)
+    last = (((1,), (1,)), ((), ()))
+    for s in range(2):
+        moved = lax.dot_general(
+            kern[:, s * BLOCK : (s + 1) * BLOCK], deltas[s], last, preferred_element_type=F32
+        )
+        total = total - moved[:, :count]
+    rest[...] = total
+    stores = [pltpu.make_async_copy(rest, residual, store_sems.at[5])]
+    stores[0].start()
+    held = [jnp.where(block_ids[s] == holder, 1.0, 0.0) for s in range(2)]
+    for i in range(5):
+        added = [deltas[s, parts[i], :].astype(F32) * held[s] for s in range(2)]
+        fetches[i].wait()
+        new_tiles[i] = old_tiles[i] + (added[0] + added[1])
+        stores.append(pltpu.make_async_copy(new_tiles.at[i], new.at[parts[i]], store_sems.at[i]))
+        stores[-1].start()
+    for store in stores:
+        store.wait()
+
+
+def finish(block_ids, kern, deltas, labels, scores, coefficients):
+    vmem = pl.BlockSpec(memory_space=pltpu.VMEM)
+    hbm = pl.BlockSpec(memory_space=pltpu.HBM)
+    count = scores.shape[1]
+    return pl.pallas_call(
+        finish_kernel,
+        out_shape=(
+            jax.ShapeDtypeStruct(coefficients.shape, F32),
+            jax.ShapeDtypeStruct(scores.shape, F32),
+        ),
+        in_specs=[pl.BlockSpec(memory_space=pltpu.SMEM)] + [vmem] * 4 + [hbm],
+        out_specs=(hbm,) * 2,
+        scratch_shapes=[
+            pltpu.VMEM((5, count // 5, BLOCK), F32),
+            pltpu.VMEM((5, count // 5, BLOCK), F32),
+            pltpu.VMEM(scores.shape, F32),
+            pltpu.SemaphoreType.DMA((5,)),
+            pltpu.SemaphoreType.DMA((6,)),
+        ],
+        compiler_params=pltpu.CompilerParams(vmem_limit_bytes=VMEM_LIMIT),
+        name="finish",
+    )(block_ids, kern, deltas, labels, scores, coefficients)
+
+
 def shards(features, labels, scores, landmarks, coefficients, block_ids):
-    count = coefficients.shape[1]
     devices_all = lax.axis_size("rows") * lax.axis_size("rrep")
     ridge = float(features.shape[0] * devices_all)
-    holder = lax.axis_index("rows")
-    classes = jnp.arange(count, dtype=jnp.int32)
-    residual = (labels[:, None] == classes[None, :]).astype(F32) - scores.astype(F32)
-    kern, deltas = update(block_ids, landmarks, features, labels[:, None], scores, ridge)
-    deltas = deltas.reshape(2, CLASSES, BLOCK)[:, :count]
-    new_coefficients = coefficients
-    for step in range(2):
-        added = jnp.where(holder == block_ids[step], deltas[step].T.astype(F32), 0.0)
-        new_coefficients = new_coefficients + added
-        residual = residual - lax.dot_general(
-            kern[:, step * BLOCK : (step + 1) * BLOCK],
-            deltas[step],
-            (((1,), (1,)), ((), ())),
-            preferred_element_type=F32,
-        )
-    return (new_coefficients, residual)
+    labels = labels[None, :]
+    kern, deltas = update(block_ids, landmarks, features, labels, scores, ridge)
+    deltas = deltas.reshape(2, CLASSES, BLOCK)
+    new, residual = finish(block_ids, kern, deltas, labels, scores, coefficients.T)
+    return new.T, residual
 
 
 def solution(mesh):

time: 134 us -> 130 us (0.970)
  Pallas kernels: 122 us -> 126 us
  matrix products: 3.24 us -> 0 us
  other arithmetic: 1.75 us -> 0 us
  local copies, waits for them, and re-layouts: 4.77 us -> 3.32 us
  between operations: 2.01 us -> 0.66 us
    pallas_call x0 -> x1, Pallas kernels: none -> 4.8 us  [finish(): pl.pallas_call(finish_kernel, out_shape=(jax.ShapeDtypeStruct(coefficient...]
    dot_general x2 -> x0, matrix products: 3.24 us -> none  [shards(): lax.dot_general(kern[:, step * BLOCK:(step + 1) * BLOCK], deltas[step], (...]
    add x1 -> x0, other arithmetic: 1.75 us -> none  [shards(): new_coefficients = new_coefficients + added]
    unnamed x12 -> x10, local copies, waits for them, and re-layouts: 2.66 us -> 3.32 us
where the time goes in v4:
time: 130 us
  Pallas kernels  126 us (97%)
  local copies, waits for them, and re-layouts  3.32 us (3%)
    pallas_call x1, Pallas kernels, update(): pl.pallas_call(functools.partial(update_kernel, ridge), out_shape=(jax.Sh...  121 us
    pallas_call x1, Pallas kernels, finish(): pl.pallas_call(finish_kernel, out_shape=(jax.ShapeDtypeStruct(coefficient...  4.8 us
    unnamed x10, local copies, waits for them, and re-layouts  3.32 us

profile of v4, /device:TPU:1, one launch (start us, length us, event | category | flops | bytes accessed | tf_op | source)
XLA Modules:
  0.0 130.2 jit_solution(8407270079892400120)
XLA Ops:
  0.6 0.0 copy-start
  0.6 1.0 copy-done
  1.6 0.0 copy-start.2
  1.6 1.0 copy-done.2
  2.6 0.0 copy-start.3
  2.6 0.7 copy-done.3
  3.3 0.0 copy-start.4
  3.3 0.7 copy-done.4
  4.0 0.0 copy-start.1
  4.0 121.4 %update.1 = (bf16[192,1024]{1,0:T(8,128)(2,1)S(1)}, bf16[2,4,4,64,512]{4,3,2,1,0:T(8,128)(2,1)}) custom-call(s32[2]{0:T(128)S(1)} %copy-done.4, bf16[512,1024]{1,0:T(8,128)(2,1)} %lands_all.1, bf16[192,1024]{1,0:T(8,128)(2,1)S(1)} %copy-done.2, s32[1,192]{1,0:T(1,128)S(1)} %bitcast.4, bf16[192,1000]{1,0:T(8,128)(2,1)S(1)} %copy-done), custom_call_target="tpu_custom_call" | custom-call | tf_op jit(solution)/shard_map/update/pallas_call | solution.py:491
  125.4 0.0 copy-done.1
  125.4 4.8 %finish.1 = (f32[1000,512]{1,0:T(8,128)}, f32[192,1000]{1,0:T(8,128)}) custom-call(s32[2]{0:T(128)S(1)} %copy-done.4, bf16[192,1024]{1,0:T(8,128)(2,1)S(1)} %get-tuple-element.6.kern, bf16[2,1024,512]{2,1,0:T(8,128)(2,1)} %bitcast.6, s32[1,192]{1,0:T(1,128)S(1)} %bitcast.5, bf16[192,1000]{1,0:T(8,128)(2,1)S(1)} %copy-done.1, f32[1000,512]{1,0:T(8,128)} %bitcast.7), custom_call_target="tpu_custom_call" | custom-call | tf_op jit(solution)/shard_map/finish/pallas_call | solution.py:593
Async XLA Ops:
  0.6 1.0 copy-start
  1.6 1.0 copy-start.2
  2.6 0.7 copy-start.3
  3.3 0.7 copy-start.4
  4.0 121.4 %copy-start.1 = (bf16[192,1000]{1,0:T(8,128)(2,1)S(1)}, bf16[192,1000]{1,0:T(8,128)(2,1)}, u32[]{:S(2)}) copy-start(bf16[192,1000]{1,0:T(8,128)(2,1)} %scores.1) | copy-start | bytes 1152004

commit v5 on v4

--- a/solution.py
+++ b/solution.py
@@ -14,8 +14,10 @@
 NX, NY, NZ = 4, 4, 8
 BLOCK = 512
 CLASSES = 1024
-VMEM_LIMIT = 52 * 2**20
+VMEM_LIMIT = 62 * 2**20
 COPIES = 138
+FAR_Z = (4, 3, 5, 2, 6, 1, 7)
+FAR = (2, 1, 3)
 TILE = 128
 TILES = BLOCK // TILE
 BELOW = [(i, j) for i in range(TILES) for j in range(i)]
@@ -48,11 +50,11 @@
         barrier = pltpu.get_barrier_semaphore()
         peers = []
         if "x" in axes:
-            peers += [self.at_x(d)[1] for d in range(1, NX)]
+            peers += [self.at_x(d)[1] for d in FAR]
         if "y" in axes:
-            peers += [self.at_y(d)[1] for d in range(1, NY)]
+            peers += [self.at_y(d)[1] for d in FAR]
         if "z" in axes:
-            peers += [self.at_z(d)[1] for d in range(1, NZ)]
+            peers += [self.at_z(d)[1] for d in FAR_Z]
         if "c" in axes:
             peers += [self.partner()]
         for peer in peers:
@@ -130,7 +132,7 @@
 def gather_landmarks(me, out, zin, rows, fetches, xin, rin, zall, xp, rp, r1, s1, r2):
     x, y, z, c = me.x, me.y, me.z, me.c
     first = []
-    for d in range(1, NY):
+    for d in FAR:
         other, device = me.at_y(d)
         first.append(out.start(zin.at[other], r1.at[d - 1], device))
     for fetch in fetches:
@@ -140,17 +142,17 @@
     arrive(first)
     s1[...] = zin[y] + r1[0] + r1[1] + r1[2]
     second = []
-    for d in range(1, NZ):
+    for d in FAR_Z:
         other, device = me.at_z(d)
         second.append(out.start(s1.at[other], r2.at[d - 1], device))
     arrive(second)
     total = s1[z]
-    for d in range(1, NZ):
+    for d in FAR_Z:
         total = total + r2[d - 1]
     s, g = z // 4, z % 4
     zall[y, s, x, c, g] = total
     mine = zall.at[y, s, x, c, g]
-    arrive([out.start(mine, mine, me.at_z(d)[1]) for d in range(1, NZ)])
+    arrive([out.start(mine, mine, me.at_z(d)[1]) for d in FAR_Z])
     spread_plane(
         me,
         out,
@@ -165,23 +167,23 @@
 def spread_plane(me, out, one_a, one_b, column, row):
     x, y = me.x, me.y
     copies = []
-    for d in range(1, 4):
+    for d in FAR:
         copies.append(out.start(one_a(x, y), one_a(x, y), me.at_y(d)[1]))
         copies.append(out.start(one_b(x, y), one_b(x, y), me.at_x(d)[1]))
     arrive(copies)
-    copies = []
-    for d in range(1, 4):
-        copies.append(out.start(column(x), column(x), me.at_x(d)[1]))
-        copies.append(out.start(row(y), row(y), me.at_y(d)[1]))
+    columns, rows = {}, {}
+    for d in FAR:
+        columns[d] = out.start(column(x), column(x), me.at_x(d)[1])
+        rows[d] = out.start(row(y), row(y), me.at_y(d)[1])
     across = [
         out.start(column(x), column(x), me.partner()),
         out.start(row(y), row(y), me.partner()),
     ]
-    for d in range(1, 4):
-        arrive([copies[2 * d - 2]])
+    for d in (1, 3, 2):
+        arrive([columns[d]])
         source = (x - d) % NX
         across.append(out.start(column(source), column(source), me.partner()))
-        arrive([copies[2 * d - 1]])
+        arrive([rows[d]])
         source = (y - d) % NY
         across.append(out.start(row(source), row(source), me.partner()))
     arrive(across)
@@ -252,7 +254,7 @@
 
 def sum_plane_one(me, out, src, ra, rb, h):
     copies = []
-    for d in range(1, 4):
+    for d in FAR:
         i, device = me.at_x(d)
         copies.append(out.start(src.at[i, :, 0:h], ra.at[d - 1], device))
         i, device = me.at_y(d)
@@ -262,7 +264,7 @@
 
 def sum_plane_two(me, out, sa, sb, ra, rb):
     copies = []
-    for d in range(1, 4):
+    for d in FAR:
         i, device = me.at_y(d)
         copies.append(out.start(sa.at[i], ra.at[d - 1], device))
         i, device = me.at_x(d)
@@ -272,7 +274,7 @@
 
 def sum_line(me, out, src, received):
     copies = []
-    for d in range(1, NZ):
+    for d in FAR_Z:
         i, device = me.at_z(d)
         copies.append(out.start(src.at[i], received.at[d - 1], device))
     return copies
@@ -403,7 +405,7 @@
     partial_grams(me, kern, gin, diag)
 
     grams = sum_plane_one(me, out, gin, ga1, gb1, 4)
-    diags = [out.start(diag, dx.at[d - 1], me.at_x(d)[1]) for d in range(1, NX)]
+    diags = [out.start(diag, dx.at[d - 1], me.at_x(d)[1]) for d in FAR]
     kout[...] = kern[:rows, :]
     partial_products(me, kern, rin, rp, pin)
     arrive(grams)
@@ -412,7 +414,7 @@
     grams = sum_plane_two(me, out, ga, gb, ga2, gb2)
     arrive(diags)
     dxs[...] = total_of(diag[...], dx)
-    diags = [out.start(dxs, dy.at[d - 1], me.at_y(d)[1]) for d in range(1, NY)]
+    diags = [out.start(dxs, dy.at[d - 1], me.at_y(d)[1]) for d in FAR]
     arrive(grams)
     g2[0:4] = total_of(ga[y], ga2)
     g2[4:8] = total_of(gb[x], gb2)
@@ -420,14 +422,14 @@
     products = sum_plane_one(me, out, pin, pa1, pb1, 32)
     arrive(diags)
     dys[...] = total_of(dxs[...], dy)
-    diags = [out.start(dys, dz.at[d - 1], me.at_z(d)[1]) for d in range(1, NZ)]
+    diags = [out.start(dys, dz.at[d - 1], me.at_z(d)[1]) for d in FAR_Z]
     arrive(grams)
     gall[x, y, z] = total_of(g2[z], g3)
     mine = gall.at[x, y, z]
-    grams = [out.start(mine, mine, me.at_z(d)[1]) for d in range(1, NZ)]
+    grams = [out.start(mine, mine, me.at_z(d)[1]) for d in FAR_Z]
     arrive(grams)
     grams = []
-    for d in range(1, 4):
+    for d in FAR:
         grams.append(out.start(gall.at[x, y, 0:4], gall.at[x, y, 0:4], me.at_y(d)[1]))
         grams.append(out.start(gall.at[x, y, 4:8], gall.at[x, y, 4:8], me.at_x(d)[1]))
     arrive(products)
@@ -435,7 +437,7 @@
     pb[...] = total_of(pin[:, y, 32:64], pb1)
     arrive(grams)
     grams = []
-    for d in range(1, 4):
+    for d in FAR:
         grams.append(out.start(gall.at[x, :, 0:4], gall.at[x, :, 0:4], me.at_x(d)[1]))
         grams.append(out.start(gall.at[:, y, 4:8], gall.at[:, y, 4:8], me.at_y(d)[1]))
     products = sum_plane_two(me, out, pa, pb, pa2, pb2)
@@ -448,7 +450,7 @@
     p2[0:4] = total_of(pa[y], pa2).reshape(4, 8, BLOCK)
     p2[4:8] = total_of(pb[x], pb2).reshape(4, 8, BLOCK)
     products = sum_line(me, out, p2, p3)
-    returns = [out.make(prod.at[z], prod.at[z], me.at_z(d)[1]) for d in range(1, NZ)]
+    returns = [out.make(prod.at[z], prod.at[z], me.at_z(d)[1]) for d in FAR_Z]
 
     def halfway():
         arrive(products)

time: 130 us -> 125 us (0.962)
  local copies, waits for them, and re-layouts: 3.32 us -> 0 us
  Pallas kernels: 126 us -> 124 us
    unnamed x10 -> x0, local copies, waits for them, and re-layouts: 3.32 us -> none
    pallas_call x1, Pallas kernels: 121 us -> 120 us  [update(): pl.pallas_call(functools.partial(update_kernel, ridge), out_shape=(jax.Sh...]
where the time goes in v5:
time: 125 us
  Pallas kernels  124 us (99%)
    pallas_call x1, Pallas kernels, update(): pl.pallas_call(functools.partial(update_kernel, ridge), out_shape=(jax.Sh...  120 us
    pallas_call x1, Pallas kernels, finish(): pl.pallas_call(finish_kernel, out_shape=(jax.ShapeDtypeStruct(coefficient...  4.29 us

profile of v5, /device:TPU:1, one launch (start us, length us, event | category | flops | bytes accessed | tf_op | source)
XLA Modules:
  0.0 125.0 jit_solution(994930218261765771)
XLA Ops:
  0.6 119.9 %update.1 = (bf16[192,1024]{1,0:T(8,128)(2,1)}, bf16[2,4,4,64,512]{4,3,2,1,0:T(8,128)(2,1)}) custom-call(s32[2]{0:T(128)} %block_ids.3, bf16[512,1024]{1,0:T(8,128)(2,1)} %lands_all.1, bf16[192,1024]{1,0:T(8,128)(2,1)} %features_all.1, s32[1,192]{1,0:T(1,128)} %bitcast.6, bf16[192,1000]{1,0:T(8,128)(2,1)} %scores.1), custom_call_target="tpu_custom_call" | custom-call | tf_op jit(solution)/shard_map/update/pallas_call | solution.py:493
  120.5 4.3 %finish.1 = (f32[1000,512]{1,0:T(8,128)}, f32[192,1000]{1,0:T(8,128)}) custom-call(s32[2]{0:T(128)} %block_ids.3, bf16[192,1024]{1,0:T(8,128)(2,1)} %get-tuple-element.6.kern, bf16[2,1024,512]{2,1,0:T(8,128)(2,1)} %bitcast.4, s32[1,192]{1,0:T(1,128)} %bitcast.7, bf16[192,1000]{1,0:T(8,128)(2,1)} %scores.1, f32[1000,512]{1,0:T(8,128)} %bitcast.5), custom_call_target="tpu_custom_call" | custom-call | tf_op jit(solution)/shard_map/finish/pallas_call | solution.py:595

commit v6 on v5

--- a/solution.py
+++ b/solution.py
@@ -63,12 +63,12 @@
 
 
 class Sender:
-    def __init__(self, send_sems, recv_sems):
+    def __init__(self, send_sems, recv_sems, base=0):
         self.send_sems, self.recv_sems = send_sems, recv_sems
-        self.copies = []
+        self.base, self.copies = base, []
 
     def make(self, src, dst, device):
-        i = len(self.copies)
+        i = self.base + len(self.copies)
         copy = pltpu.make_async_remote_copy(
             src_ref=src,
             dst_ref=dst,
@@ -461,26 +461,42 @@
     invert(inv, pivots, halfway)
     arrive(returns)
 
-    target = prod[...].reshape(64, BLOCK)
-    first = jnp.dot(target, inv[...], **EXACT)
-    delta[...] = first
-    swap = [out.start(delta, other, me.partner())]
-    part[...] = cross_product(first, side[...])
-    swap.append(out.start(part, opart, me.partner()))
-    arrive(swap[:1])
-    here = cross_product(other[...], side[...])
-    arrive(swap[1:])
-    cross = jnp.concatenate([opart[...], here], axis=1)
-    second = jnp.dot(target - cross, inv[...], **EXACT)
-    dout[c, x, y] = jnp.where(c == 0, first, second).astype(BF16)
-    spread_plane(
-        me,
-        out,
-        lambda i, j: dout.at[c, i, j, 0:32],
-        lambda i, j: dout.at[c, i, j, 32:64],
-        lambda i: dout.at[c, i, :, 0:32],
-        lambda j: dout.at[c, :, j, 32:64],
-    )
+    used = len(out.copies)
+    gifts = Sender(send_sems, recv_sems, used)
+    gifts.make(delta, other, me.partner())
+    gifts.make(part, opart, me.partner())
+
+    def share(value):
+        last = Sender(send_sems, recv_sems, used + 2)
+        dout[c, x, y] = value.astype(BF16)
+        spread_plane(
+            me,
+            last,
+            lambda i, j: dout.at[c, i, j, 0:32],
+            lambda i, j: dout.at[c, i, j, 32:64],
+            lambda i: dout.at[c, i, :, 0:32],
+            lambda j: dout.at[c, :, j, 32:64],
+        )
+        last.drain()
+
+    @pl.when(c == 0)
+    def _():
+        first = jnp.dot(prod[...].reshape(64, BLOCK), inv[...], **EXACT)
+        delta[...] = first
+        gifts.copies[0].start()
+        part[...] = cross_product(first, side[...])
+        gifts.copies[1].start()
+        share(first)
+        gifts.drain()
+
+    @pl.when(c == 1)
+    def _():
+        arrive(gifts.copies[:1])
+        here = cross_product(other[...], side[...])
+        arrive(gifts.copies[1:])
+        cross = jnp.concatenate([opart[...], here], axis=1)
+        share(jnp.dot(prod[...].reshape(64, BLOCK) - cross, inv[...], **EXACT))
+
     out.drain()
 
 

time: 125 us -> 123 us (0.984)
    pallas_call x1, Pallas kernels: 120 us -> 118 us  [update(): pl.pallas_call(functools.partial(update_kernel, ridge), out_shape=(jax.Sh...]
where the time goes in v6:
time: 123 us
  Pallas kernels  123 us (100%)
    pallas_call x1, Pallas kernels, update(): pl.pallas_call(functools.partial(update_kernel, ridge), out_shape=(jax.Sh...  118 us
    pallas_call x1, Pallas kernels, finish(): pl.pallas_call(finish_kernel, out_shape=(jax.ShapeDtypeStruct(coefficient...  4.29 us

profile of v6, /device:TPU:1, one launch (start us, length us, event | category | flops | bytes accessed | tf_op | source)
XLA Modules:
  0.0 123.3 jit_solution(6150407514513957933)
XLA Ops:
  0.6 118.3 %update.1 = (bf16[192,1024]{1,0:T(8,128)(2,1)}, bf16[2,4,4,64,512]{4,3,2,1,0:T(8,128)(2,1)}) custom-call(s32[2]{0:T(128)} %block_ids.3, bf16[512,1024]{1,0:T(8,128)(2,1)} %lands_all.1, bf16[192,1024]{1,0:T(8,128)(2,1)} %features_all.1, s32[1,192]{1,0:T(1,128)} %bitcast.6, bf16[192,1000]{1,0:T(8,128)(2,1)} %scores.1), custom_call_target="tpu_custom_call" | custom-call | tf_op jit(solution)/shard_map/update/pallas_call | solution.py:509
  119.0 4.3 %finish.1 = (f32[1000,512]{1,0:T(8,128)}, f32[192,1000]{1,0:T(8,128)}) custom-call(s32[2]{0:T(128)} %block_ids.3, bf16[192,1024]{1,0:T(8,128)(2,1)} %get-tuple-element.6.kern, bf16[2,1024,512]{2,1,0:T(8,128)(2,1)} %bitcast.4, s32[1,192]{1,0:T(1,128)} %bitcast.7, bf16[192,1000]{1,0:T(8,128)(2,1)} %scores.1, f32[1000,512]{1,0:T(8,128)} %bitcast.5), custom_call_target="tpu_custom_call" | custom-call | tf_op jit(solution)/shard_map/finish/pallas_call | solution.py:611

commit v7 on v6

--- a/solution.py
+++ b/solution.py
@@ -435,12 +435,12 @@
     arrive(products)
     pa[...] = total_of(pin[x, :, 0:32], pa1)
     pb[...] = total_of(pin[:, y, 32:64], pb1)
+    products = sum_plane_two(me, out, pa, pb, pa2, pb2)
     arrive(grams)
     grams = []
     for d in FAR:
         grams.append(out.start(gall.at[x, :, 0:4], gall.at[x, :, 0:4], me.at_x(d)[1]))
         grams.append(out.start(gall.at[:, y, 4:8], gall.at[:, y, 4:8], me.at_y(d)[1]))
-    products = sum_plane_two(me, out, pa, pb, pa2, pb2)
     arrive(diags)
     lost = total_of(dys[...], dz)
     arrive(grams)

time: 123 us -> 123 us (level)
  no operation moved by 1% of the time
where the time goes in v7:
time: 123 us
  Pallas kernels  122 us (99%)
    pallas_call x1, Pallas kernels, update(): pl.pallas_call(functools.partial(update_kernel, ridge), out_shape=(jax.Sh...  118 us
    pallas_call x1, Pallas kernels, finish(): pl.pallas_call(finish_kernel, out_shape=(jax.ShapeDtypeStruct(coefficient...  4.29 us

profile of v7, /device:TPU:1, one launch (start us, length us, event | category | flops | bytes accessed | tf_op | source)
XLA Modules:
  0.0 122.6 jit_solution(611039248367130735)
XLA Ops:
  0.6 117.6 %update.1 = (bf16[192,1024]{1,0:T(8,128)(2,1)}, bf16[2,4,4,64,512]{4,3,2,1,0:T(8,128)(2,1)}) custom-call(s32[2]{0:T(128)} %block_ids.3, bf16[512,1024]{1,0:T(8,128)(2,1)} %lands_all.1, bf16[192,1024]{1,0:T(8,128)(2,1)} %features_all.1, s32[1,192]{1,0:T(1,128)} %bitcast.6, bf16[192,1000]{1,0:T(8,128)(2,1)} %scores.1), custom_call_target="tpu_custom_call" | custom-call | tf_op jit(solution)/shard_map/update/pallas_call | solution.py:509
  118.3 4.3 %finish.1 = (f32[1000,512]{1,0:T(8,128)}, f32[192,1000]{1,0:T(8,128)}) custom-call(s32[2]{0:T(128)} %block_ids.3, bf16[192,1024]{1,0:T(8,128)(2,1)} %get-tuple-element.6.kern, bf16[2,1024,512]{2,1,0:T(8,128)(2,1)} %bitcast.4, s32[1,192]{1,0:T(1,128)} %bitcast.7, bf16[192,1000]{1,0:T(8,128)(2,1)} %scores.1, f32[1000,512]{1,0:T(8,128)} %bitcast.5), custom_call_target="tpu_custom_call" | custom-call | tf_op jit(solution)/shard_map/finish/pallas_call | solution.py:611
